TPU v7x, 128 devices: a whole 4x4x4 slice. The times are simulated.
128 devices in a mesh: row: 4 (over z), kv: 32 (over x, y, core).
Axes of the slice: x: 4, y: 4, z: 4, core: 2. Of those that a mesh axis runs over, the one named last changes fastest.
Arguments:
- hidden: bfloat16 [256, 5120], P(None, 'kv'), may hold values from -6 to 6
- query_weight: bfloat16 [5120, 8192], P('kv', 'row'), may hold values from -0.078125 to 0.078125
- adapter_down_weight: bfloat16 [32, 5120, 16], P(None, 'kv'), may hold values from -0.078125 to 0.078125
- adapter_up_weight: float32 [32, 16, 8192], P(None, None, 'row'), may hold values from -1.5 to 1.5
- query_norm_gain: float32 [128], replicated, may hold values from 0.1 to 1.9
- paged_key_cache: bfloat16 [4096, 128, 8, 128], P('kv', None, 'row'), may hold values from -400 to 400
- paged_value_cache: bfloat16 [4096, 128, 8, 128], P('kv', None, 'row'), may hold values from -6 to 6
- output_weight: bfloat16 [8192, 5120], P('row', 'kv'), may hold values from -0.0625 to 0.0625
- holder: int32 [256, 32], P('kv'), may hold values from 0 to 31, as said below
- holder_block_index: int32 [256, 32], P('kv'), may hold values from 0 to 127
- block_used_length: int32 [256, 32], P('kv'), may hold values from 1 to 128
- tenant: int32 [256], replicated, may hold values from 0 to 63
- tenant_adapter: int32 [64], replicated, may hold values from 0 to 31
Outputs:
- projected: bfloat16 [256, 5120], P('row', 'kv')
Inputs may be any that keep to these rules, and one draw needn't show every extreme that they name: At most 16 of the 8 x 32 slots of the rows of one index of kv name one holder; in every draw one holder is named exactly 16 times by the slots of every index.
All inputs are finite; a program needn't handle non-finite values.
Results may differ from a plain program's by a relative error of at most 0.0159.
The roundings to bfloat16 on the way count: a program that leaves them out, or rounds other values in their place, can miss the bound.
Values may be sent and summed in bfloat16 or wider, within the bound.
A program may use at most 256 MiB of HBM per device.

v0:
```python
import math

import jax
import jax.numpy as jnp
from jax import lax
from jax.sharding import PartitionSpec as P

ADAPTER_SCALE = 0.5
ROPE_BASE = 1000000.0
EPSILON = 1e-06
NEG_FILL = -1e30


def rotate_half(query, position):
    half_width = query.shape[-1] // 2
    frequency = ROPE_BASE ** (-(jnp.arange(half_width, dtype=jnp.float32) * 2.0) / query.shape[-1])
    angles = position[:, None] * frequency[None, :]
    cosine = jnp.concatenate([jnp.cos(angles), jnp.cos(angles)], axis=-1)[:, None, :]
    sine_part = jnp.concatenate([jnp.sin(angles), jnp.sin(angles)], axis=-1)[:, None, :]
    first_half = query[..., :half_width]
    second_half = query[..., half_width:]
    turned = jnp.concatenate([-second_half, first_half], axis=-1)
    return query * cosine + turned * sine_part


def prepare_queries(query_linear, query_norm_gain, block_used_length):
    row_count = query_linear.shape[0]
    head_size = query_norm_gain.shape[0]
    query = query_linear.reshape(row_count, query_linear.shape[1] // head_size, head_size)
    squares = jnp.mean(query * query, axis=-1, keepdims=True)
    query = query * lax.rsqrt(squares + EPSILON) * query_norm_gain
    position = (jnp.sum(block_used_length, axis=1) - 1).astype(jnp.float32)
    return rotate_half(query, position).astype(jnp.bfloat16)


def merge_blocks(block_out, block_top, block_total, axis):
    overall = jnp.max(block_top, axis=axis, keepdims=True)
    factors = jnp.exp(block_top - overall)
    numerator = jnp.sum(factors[..., None] * block_out, axis=axis)
    denominator = jnp.sum(factors * block_total, axis=axis)
    return numerator / denominator[..., None]


def local(
    hidden,
    query_weight,
    adapter_down_weight,
    adapter_up_weight,
    query_norm_gain,
    paged_key_cache,
    paged_value_cache,
    output_weight,
    holder,
    holder_block_index,
    block_used_length,
    tenant,
    tenant_adapter,
):
    own_rows = holder.shape[0]
    slot_count = holder.shape[1]
    kv_count = lax.axis_size("kv")
    my_index = lax.axis_index("kv")
    adapter_total = adapter_down_weight.shape[0]
    adapter_rank_size = adapter_down_weight.shape[2]
    query_width = query_weight.shape[1]
    head_size = query_norm_gain.shape[0]
    local_blocks = paged_key_cache.shape[0]
    kv_local = paged_key_cache.shape[2]
    block_size = paged_key_cache.shape[1]
    group_size = query_width // (kv_local * head_size)
    flat_keys = paged_key_cache.reshape(local_blocks, block_size * kv_local * head_size)
    flat_values = paged_value_cache.reshape(local_blocks, block_size * kv_local * head_size)
    tenant_match = tenant[:, None] == jnp.arange(tenant_adapter.shape[0], dtype=jnp.int32)[None, :]
    adapter_per_row = jnp.sum(jnp.where(tenant_match, tenant_adapter[None, :], 0), axis=1)
    adapter_match = (
        adapter_per_row[:, None] == jnp.arange(adapter_total, dtype=jnp.int32)[None, :]
    ).astype(jnp.float32)
    up_weight_flat = adapter_up_weight.reshape(adapter_total * adapter_rank_size, query_width)
    query_linear = lax.psum_scatter(
        jnp.dot(hidden, query_weight, preferred_element_type=jnp.float32),
        "kv",
        scatter_dimension=0,
        tiled=True,
    )
    partial_low = jnp.sum(
        jnp.einsum("ib,xbz->ixz", hidden, adapter_down_weight, preferred_element_type=jnp.float32)
        * adapter_match[:, :, None],
        axis=1,
    )
    own_low = lax.psum_scatter(partial_low, "kv", scatter_dimension=0, tiled=True)
    own_match = lax.dynamic_slice_in_dim(adapter_match, my_index * own_rows, own_rows, 0)
    spread = (own_low[:, None, :] * own_match[:, :, None]).reshape(
        own_rows, adapter_total * adapter_rank_size
    )
    query_linear = query_linear + ADAPTER_SCALE * jnp.dot(
        spread, up_weight_flat, precision=lax.Precision.HIGHEST, preferred_element_type=jnp.float32
    )
    queries = prepare_queries(query_linear, query_norm_gain, block_used_length).reshape(
        own_rows, query_width
    )
    entry_count = own_rows * slot_count
    capacity = 2 * entry_count // kv_count
    slot_total = kv_count * capacity
    slot_ids = jnp.arange(slot_total, dtype=jnp.int32)
    destination = holder.reshape(entry_count)
    dest_match = (destination[:, None] == jnp.arange(kv_count, dtype=jnp.int32)[None, :]).astype(
        jnp.int32
    )
    earlier = jnp.cumsum(dest_match, axis=0) - dest_match
    position = jnp.sum(earlier * dest_match, axis=1)
    slot_index = destination * capacity + position
    slot_match = slot_index[None, :] == slot_ids[:, None]
    row_pick = jnp.any(slot_match.reshape(slot_total, own_rows, slot_count), axis=2).astype(
        jnp.bfloat16
    )
    sent_queries = jnp.dot(row_pick, queries, preferred_element_type=jnp.bfloat16).reshape(
        kv_count, capacity, query_width
    )
    entry_fields = jnp.stack(
        [holder_block_index.reshape(entry_count), block_used_length.reshape(entry_count)], axis=1
    )
    sent_fields = jnp.sum(
        jnp.where(slot_match[:, :, None], entry_fields[None, :, :], 0), axis=1
    ).reshape(kv_count, capacity, 2)
    received_queries = lax.all_to_all(sent_queries, "kv", split_axis=0, concat_axis=0, tiled=True)
    received_fields = lax.all_to_all(sent_fields, "kv", split_axis=0, concat_axis=0, tiled=True)
    source_count = received_queries.shape[0]
    item_count = received_queries.shape[1]
    total_items = source_count * item_count
    blocks = received_fields[..., 0].reshape(total_items)
    lengths = received_fields[..., 1].reshape(total_items)
    block_pick = (blocks[:, None] == jnp.arange(local_blocks, dtype=jnp.int32)[None, :]).astype(
        jnp.bfloat16
    )
    keys = jnp.dot(block_pick, flat_keys, preferred_element_type=jnp.bfloat16).reshape(
        total_items, block_size, kv_local, head_size
    )
    values = jnp.dot(block_pick, flat_values, preferred_element_type=jnp.bfloat16).reshape(
        total_items, block_size, kv_local, head_size
    )
    grouped = received_queries.reshape(total_items, kv_local, group_size, head_size)
    scores = jnp.einsum("rajd,rtad->rajt", grouped, keys, preferred_element_type=jnp.float32) * (
        1.0 / math.sqrt(head_size)
    )
    token_mask = (jnp.arange(block_size, dtype=jnp.int32)[None, :] < lengths[:, None])[
        :, None, None, :
    ]
    block_top = jnp.max(jnp.where(token_mask, scores, NEG_FILL), axis=-1)
    weights = jnp.where(token_mask, jnp.exp(scores - block_top[..., None]), 0.0)
    block_total = jnp.sum(weights, axis=-1)
    block_out = jnp.einsum(
        "rajt,rtad->rajd", weights.astype(jnp.bfloat16), values, preferred_element_type=jnp.float32
    )
    lead = (source_count, item_count, kv_local, group_size)
    block_out, block_top, block_total = (
        block_out.reshape(lead + (head_size,)),
        block_top.reshape(lead),
        block_total.reshape(lead),
    )
    returned = (
        lax.all_to_all(block_out, "kv", split_axis=0, concat_axis=0, tiled=True),
        lax.all_to_all(block_top, "kv", split_axis=0, concat_axis=0, tiled=True),
        lax.all_to_all(block_total, "kv", split_axis=0, concat_axis=0, tiled=True),
    )
    slot_weight = slot_match.astype(jnp.float32)
    picked = []
    for piece in returned:
        trailing = piece.shape[2:]
        flat_piece = piece.reshape(slot_total, -1)
        chosen = jnp.dot(
            slot_weight.T,
            flat_piece,
            precision=lax.Precision.HIGHEST,
            preferred_element_type=jnp.float32,
        )
        picked.append(chosen.reshape((own_rows, slot_count) + trailing))
    attended = merge_blocks(picked[0], picked[1], picked[2], 1)
    attention = attended.reshape(own_rows, query_width).astype(jnp.bfloat16)
    terms = jnp.dot(
        lax.all_gather(attention, "kv", axis=0, tiled=True),
        output_weight,
        preferred_element_type=jnp.float32,
    )
    return lax.psum_scatter(terms.astype(jnp.bfloat16), "row", scatter_dimension=0, tiled=True)


def solution(mesh):
    return jax.shard_map(
        local,
        mesh=mesh,
        in_specs=(
            P(None, "kv"),
            P("kv", "row"),
            P(None, "kv", None),
            P(None, None, "row"),
            P(),
            P("kv", None, "row", None),
            P("kv", None, "row", None),
            P("row", "kv"),
            P("kv", None),
            P("kv", None),
            P("kv", None),
            P(),
            P(),
        ),
        out_specs=P("row", "kv"),
        check_vma=False,
    )
```

profile of v0, /device:TPU:1, one launch (start us, length us, event | category | flops | bytes accessed | tf_op | source)
XLA Modules:
  0.0 566.3 jit_solution(4185088476070717693)
XLA Ops:
  7.7 2.7 fusion.72
  12.8 8.6 %all-to-all-start = ((s32[32,16,2]{1,2,0:T(2,128)}), s32[32,16,2]{1,2,0:T(2,128)S(1)}, u32[]{:S(2)}, u32[]{:S(2)}) async-start(s32[32,16,2]{1,2,0:T(2,128)} %copy.55), calls=%async_computation | async-start | bytes 65536 | tf_op jit(solution)/shard_map/all_to_all | solution.py:126
  23.4 123.3 %all-reduce = f32[256,16]{0,1:T(8,128)S(1)} all-reduce(f32[256,16]{0,1:T(8,128)S(1)} %fusion.22), channel_id=3, replica_groups=mesh['row'=4,'kv'=32] {'kv'}, use_global_device_ids=true, to_apply=%region_8.9.clone | all-reduce | flops 4096 | bytes 32768
  147.5 14.4 %reshape.223 = bf16[128,32768]{1,0:T(8,128)(2,1)} reshape(bf16[128,128,2,128]{3,2,1,0:T(2,128)(2,1)} %param.18) | data formatting | bytes 16777216 | tf_op jit(solution)/shard_map/reshape | solution.py:71
  161.9 11.9 %copy.60 = bf16[32768,128]{1,0:T(8,128)(2,1)} copy(bf16[32768,128]{0,1:T(8,128)(2,1)} %bitcast.152) | data formatting | bytes 16777216 | tf_op jit(solution)/shard_map/dot_general | solution.py:135
  173.8 14.4 %reshape.226 = bf16[128,32768]{1,0:T(8,128)(2,1)} reshape(bf16[128,128,2,128]{3,2,1,0:T(2,128)(2,1)} %param.19) | data formatting | bytes 16777216 | tf_op jit(solution)/shard_map/reshape | solution.py:72
  188.3 11.9 %copy.65 = bf16[32768,128]{1,0:T(8,128)(2,1)} copy(bf16[32768,128]{0,1:T(8,128)(2,1)} %bitcast.153) | data formatting | bytes 16777216 | tf_op jit(solution)/shard_map/dot_general | solution.py:138
  200.6 7.5 %fusion.49 = (f32[8,16]{0,1:T(8,128)S(1)}, f32[8,2048]{1,0:T(8,128)S(1)}) fusion(f32[8,2048]{1,0:T(8,128)} %reduce-scatter.4.cloned.1.call-done, f32[32,16,2048]{2,1,0:T(8,128)} %param.16, f32[8,32]{1,0:T(8,128)S(1)} %copy.57, f32[8,16]{0,1:T(8,128)S(1)} %constant_dynamic-slice_fusion), kind=kOutput, calls=%fused_computation.55 | convolution fusion | flops 100732800 | bytes 4327424 | tf_op jit(solution)/shard_map/dot_general | solution.py:95
  210.4 9.3 %all-to-all-start.1 = ((bf16[32,16,2048]{2,1,0:T(8,128)(2,1)}), bf16[32,16,2048]{2,1,0:T(8,128)(2,1)S(1)}, u32[]{:S(2)}, u32[]{:S(2)}) async-start(bf16[32,16,2048]{2,1,0:T(8,128)(2,1)} %fusion.42), calls=%async_computation.2 | async-start | bytes 4194304 | tf_op jit(solution)/shard_map/all_to_all | solution.py:125
  219.7 17.0 %fusion.38 = bf16[512,128,2,128]{3,0,2,1:T(8,128)(2,1)} fusion(bf16[128,2,128,128]{3,2,1,0:T(8,128)(2,1)} %bitcast.151, s32[512]{0:T(512)S(1)} %eq.138), kind=kOutput, calls=%fused_computation.39 | convolution fusion | flops 4295032832 | bytes 41945088 | tf_op jit(solution)/shard_map/dot_general | solution.py:135
  236.8 11.3 %all-to-all-done.1 = bf16[32,16,2048]{2,1,0:T(8,128)(2,1)S(1)} async-done(((bf16[32,16,2048]{2,1,0:T(8,128)(2,1)}), bf16[32,16,2048]{2,1,0:T(8,128)(2,1)S(1)}, u32[]{:S(2)}, u32[]{:S(2)}) %all-to-all-start.1) | async-done | bytes 2097184 | tf_op jit(solution)/shard_map/all_to_all | solution.py:125
  251.7 85.2 %select_reduce_fusion = (f32[512,2,8]{2,1,0:T(2,128)S(1)}, f32[512,2,8,128]{3,2,1,0:T(8,128)}) fusion(pred[512,128]{1,0:T(8,128)(4,1)S(1)} %iota_compare_fusion.4, bf16[512,2,8,128]{3,2,1,0:T(8,128)(2,1)S(1)} %bitcast.154, bf16[512,128,2,128]{3,0,2,1:T(8,128)(2,1)} %fusion.38), kind=kOutput, calls=%fused_computation.7 | convolution fusion | flops 271572992 | bytes 39944192 | tf_op jit(solution)/shard_map/rajd,rtad->rajt/dot_general | solution.py:142
  336.9 15.7 %fusion.6 = f32[512,2,8]{2,1,0:T(2,128)S(1)} fusion(f32[512,2,8,128]{3,2,1,0:T(8,128)} %get-tuple-element.14, f32[512,2,8]{2,1,0:T(2,128)S(1)} %get-tuple-element.13, pred[512,128]{1,0:T(8,128)(4,1)S(1)} %iota_compare_fusion.4), kind=kLoop, calls=%fused_computation.8 | loop fusion | flops 4186112 | bytes 4325376 | tf_op jit(solution)/shard_map/reduce_sum | solution.py:150
  353.6 4.3 all-to-all-start.4
  357.9 17.0 %fusion.36 = bf16[512,128,2,128]{3,0,2,1:T(8,128)(2,1)} fusion(bf16[128,2,128,128]{3,2,1,0:T(8,128)(2,1)} %bitcast.150, s32[512]{0:T(512)S(1)} %eq.138), kind=kOutput, calls=%fused_computation.38 | convolution fusion | flops 4295032832 | bytes 41945088 | tf_op jit(solution)/shard_map/dot_general | solution.py:138
  375.9 7.5 %all-to-all-start.2 = ((f32[32,1,256]{2,1,0:T(1,128)}), f32[32,1,256]{2,1,0:T(1,128)S(1)}, u32[]{:S(2)}, u32[]{:S(2)}) async-start(f32[32,1,256]{2,1,0:T(1,128)} %reshape.256), calls=%async_computation.3 | async-start | bytes 65536 | tf_op jit(solution)/shard_map/all_to_all | solution.py:162
  383.4 35.6 %fusion = f32[512,2,8,128]{3,2,1,0:T(8,128)} fusion(bf16[512,128,2,128]{3,0,2,1:T(8,128)(2,1)} %fusion.36, f32[512,2,8,128]{3,2,1,0:T(8,128)} %get-tuple-element.14, f32[512,2,8]{2,1,0:T(2,128)S(1)} %get-tuple-element.13, pred[512,128]{1,0:T(8,128)(4,1)S(1)} %iota_compare_fusion.4), kind=kOutput, calls=%fused_computation | convolution fusion | flops 272629760 | bytes 42041344 | tf_op jit(solution)/shard_map/rajt,rtad->rajd/dot_general | solution.py:151
  419.0 7.4 %all-to-all-start.3 = ((f32[32,16,2,8,128]{4,3,2,1,0:T(8,128)}), f32[32,16,2,8,128]{4,3,2,1,0:T(8,128)}, u32[]{:S(2)}, u32[]{:S(2)}) async-start(f32[32,16,2,8,128]{4,3,2,1,0:T(8,128)} %bitcast.157), calls=%async_computation.4 | async-start | bytes 8388608 | tf_op jit(solution)/shard_map/all_to_all | solution.py:161
  432.3 46.4 %all-to-all-done.3 = f32[32,16,2,8,128]{4,3,2,1,0:T(8,128)} async-done(((f32[32,16,2,8,128]{4,3,2,1,0:T(8,128)}), f32[32,16,2,8,128]{4,3,2,1,0:T(8,128)}, u32[]{:S(2)}, u32[]{:S(2)}) %all-to-all-start.3) | async-done | bytes 4194336 | tf_op jit(solution)/shard_map/all_to_all | solution.py:161
  478.7 4.9 reshape.228
  483.6 5.4 copy.67
  489.0 4.8 multiply_reduce_fusion
  494.6 45.1 %all-gather.2.cloned.1.call-done = bf16[256,2048]{1,0:T(8,128)(2,1)} async-done(((bf16[8,2048]{1,0:T(8,128)(2,1)}), bf16[256,2048]{1,0:T(8,128)(2,1)}) %all-gather.2.cloned.1.call-update) | async-done | bytes 1048592 | tf_op jit(solution)/shard_map/all_gather | solution.py:180
  542.0 17.5 %reduce-scatter.6.cloned.1.call-done = bf16[64,160]{1,0:T(8,128)(2,1)} async-done(((bf16[256,160]{1,0:T(8,128)(2,1)}), bf16[64,160]{1,0:T(8,128)(2,1)}) %reduce-scatter.6.cloned.1.call-update) | async-done | bytes 20496 | tf_op jit(solution)/shard_map/reduce_scatter | solution.py:184
  (97 shorter events, 22.5 us)
Async XLA Ops:
  6.5 1.2 copy-start
  6.5 15.1 %copy-start.12 = (u32[128]{0:T(128)S(1)}, u32[128]{0:T(128)}, u32[]{:S(2)}) copy-start(u32[128]{0:T(128)} %constant.49) | copy-start | bytes 1540
  6.5 16.6 %copy-start.3 = (bf16[256,160]{0,1:T(8,128)(2,1)S(1)}, bf16[256,160]{0,1:T(8,128)(2,1)}, u32[]{:S(2)}) copy-start(bf16[256,160]{0,1:T(8,128)(2,1)} %param.13) | copy-start | bytes 245764
  6.5 3.9 copy-start.4
  6.5 4.9 copy-start.6
  6.5 5.0 copy-start.5
  6.6 16.4 %copy-start.8 = (s32[256]{0:T(256)S(1)}, s32[256]{0:T(256)}, u32[]{:S(2)}) copy-start(s32[256]{0:T(256)} %param.24) | copy-start | bytes 3076
  6.6 16.4 %copy-start.9 = (s32[64]{0:T(128)S(1)}, s32[64]{0:T(128)}, u32[]{:S(2)}) copy-start(s32[64]{0:T(128)} %param.25) | copy-start | bytes 772
  6.6 16.6 %copy-start.11 = (bf16[32,160,16]{1,2,0:T(8,128)(2,1)S(1)}, bf16[32,160,16]{1,2,0:T(8,128)(2,1)}, u32[]{:S(2)}) copy-start(bf16[32,160,16]{1,2,0:T(8,128)(2,1)} %param.15) | copy-start | bytes 491524
  6.6 140.5 %copy-start.7 = (f32[128]{0:T(128)S(1)}, f32[128]{0:T(128)}, u32[]{:S(2)}) copy-start(f32[128]{0:T(128)} %param.17) | copy-start | bytes 1540
  6.6 194.0 %reduce-scatter.4.cloned.1.call-start = ((), (), s32[]{:S(2)}) async-start(), calls=%async_computation.7 | async-start | bytes 2162688 | tf_op jit(solution)/shard_map/reduce_scatter | solution.py:79
  12.8 187.4 %all-to-all-start = ((s32[32,16,2]{1,2,0:T(2,128)}), s32[32,16,2]{1,2,0:T(2,128)S(1)}, u32[]{:S(2)}, u32[]{:S(2)}) async-start(s32[32,16,2]{1,2,0:T(2,128)} %copy.55), calls=%async_computation | async-start | bytes 65536 | tf_op jit(solution)/shard_map/all_to_all | solution.py:126
  210.4 37.7 %all-to-all-start.1 = ((bf16[32,16,2048]{2,1,0:T(8,128)(2,1)}), bf16[32,16,2048]{2,1,0:T(8,128)(2,1)S(1)}, u32[]{:S(2)}, u32[]{:S(2)}) async-start(bf16[32,16,2048]{2,1,0:T(8,128)(2,1)} %fusion.42), calls=%async_computation.2 | async-start | bytes 4194304 | tf_op jit(solution)/shard_map/all_to_all | solution.py:125
  248.1 1.4 copy-start.2
  353.6 22.4 %all-to-all-start.4 = ((f32[32,1,256]{2,1,0:T(1,128)}), f32[32,1,256]{2,1,0:T(1,128)S(1)}, u32[]{:S(2)}, u32[]{:S(2)}) async-start(f32[32,1,256]{2,1,0:T(1,128)} %reshape.258), calls=%async_computation.5 | async-start | bytes 65536 | tf_op jit(solution)/shard_map/all_to_all | solution.py:163
  375.9 43.1 %all-to-all-start.2 = ((f32[32,1,256]{2,1,0:T(1,128)}), f32[32,1,256]{2,1,0:T(1,128)S(1)}, u32[]{:S(2)}, u32[]{:S(2)}) async-start(f32[32,1,256]{2,1,0:T(1,128)} %reshape.256), calls=%async_computation.3 | async-start | bytes 65536 | tf_op jit(solution)/shard_map/all_to_all | solution.py:162
  419.0 59.7 %all-to-all-start.3 = ((f32[32,16,2,8,128]{4,3,2,1,0:T(8,128)}), f32[32,16,2,8,128]{4,3,2,1,0:T(8,128)}, u32[]{:S(2)}, u32[]{:S(2)}) async-start(f32[32,16,2,8,128]{4,3,2,1,0:T(8,128)} %bitcast.157), calls=%async_computation.4 | async-start | bytes 8388608 | tf_op jit(solution)/shard_map/all_to_all | solution.py:161
  426.5 113.2 %all-gather.2.cloned.1.call-start = ((), (), s32[]{:S(2)}) async-start(), calls=%async_computation.8 | async-start | bytes 1081344 | tf_op jit(solution)/shard_map/all_gather | solution.py:180
  483.6 75.9 %copy-start.1 = (bf16[160,2048]{1,0:T(8,128)(2,1)S(1)}, bf16[160,2048]{1,0:T(8,128)(2,1)}, u32[]{:S(2)}) copy-start(bf16[160,2048]{1,0:T(8,128)(2,1)} %param.14) | copy-start | bytes 1966084
  489.0 50.7 %copy-start.10 = (bf16[2048,160]{0,1:T(8,128)(2,1)S(1)}, bf16[2048,160]{0,1:T(8,128)(2,1)}, u32[]{:S(2)}) copy-start(bf16[2048,160]{0,1:T(8,128)(2,1)} %param.20) | copy-start | bytes 1966084
  494.5 65.0 %reduce-scatter.6.cloned.1.call-start = ((), (), s32[]{:S(2)}) async-start(), calls=%async_computation.9 | async-start | bytes 163840 | tf_op jit(solution)/shard_map/reduce_scatter | solution.py:184
Sparse Core Ops, SparseCore 0:
  11.0 80.3 reduce-scatter.3
  494.6 44.9 all-gather.1
  542.1 17.3 reduce-scatter.5
where the time goes:
time: 572 us; the launch traced here: 566 us
  matrix products  176 us (31%)
  blocking collectives  123 us (22%)
  waiting for transfers between devices  120 us (21%)
  local copies, waits for them, and re-layouts  74.1 us (13%)
  starting transfers between devices  37.5 us (7%)
  other arithmetic  20.6 us (4%)
  between operations  14.4 us (3%)
    unnamed x1, blocking collectives  123 us
    dot_general x1, matrix products, local(): jnp.einsum('rajd,rtad->rajt', grouped, keys, preferred_element_type=jnp.f...  85.2 us
    all_to_all x1, waiting for transfers between devices, local(): lax.all_to_all(block_out, 'kv', split_axis=0, concat_axis=0, tiled=True)  46.4 us
    all_gather x1, waiting for transfers between devices, local(): lax.all_gather(attention, 'kv', axis=0, tiled=True)  45.1 us
    dot_general x1, matrix products, local(): jnp.einsum('rajt,rtad->rajd', weights.astype(jnp.bfloat16), values, prefe...  35.6 us
    reduce_scatter x1, waiting for transfers between devices, local(): lax.psum_scatter(terms.astype(jnp.bfloat16), 'row', scatter_dimension=0,...  17.5 us
    dot_general x1, matrix products, local(): jnp.dot(block_pick, flat_keys, preferred_element_type=jnp.bfloat16)  17 us
    dot_general x1, matrix products, local(): jnp.dot(block_pick, flat_values, preferred_element_type=jnp.bfloat16)  17 us
  transfers between devices with their start and end apart: 8, of which 4 were waited for; matrix products, arithmetic and copies ran while one was open for 24% of the time, Pallas kernels for 0%

commit v1 on v0

v1 whole, which is shorter than its diff:
```python
import functools
import math

import jax
import jax.numpy as jnp
from jax import lax
from jax.experimental import pallas as pl
from jax.experimental.pallas import tpu as pltpu
from jax.sharding import PartitionSpec as P

NEG = -1e30
F32, BF16, I32 = jnp.float32, jnp.bfloat16, jnp.int32
NT = (((1,), (1,)), ((), ()))
TN = (((0,), (0,)), ((), ()))
TT = (((0,), (1,)), ((), ()))
MESH = pl.DeviceIdType.MESH
PIECES = 8
ADAPTER_SCALE = 0.5
ROPE_BASE = 1000000.0
EPSILON = 1e-06


def iota(shape, dim):
    return lax.broadcasted_iota(I32, shape, dim)


def flat_row(x):
    rows, n = x.shape
    wide = jnp.concatenate([x.astype(F32)] * rows, axis=1)
    keep = lax.div(iota(wide.shape, 1), n) == iota(wide.shape, 0)
    return jnp.sum(jnp.where(keep, wide, 0.0), axis=0, keepdims=True)


def remote(src, dst, send, recv, device):
    return pltpu.make_async_remote_copy(
        src_ref=src, dst_ref=dst, send_sem=send, recv_sem=recv, device_id=device, device_id_type=MESH)


def project_kernel(ht_ref, w_ref, dt_ref, up_hbm, gain_ref, freq_ref, holder_ref, index_ref, used_ref,
                   tenant_ref, held_ref, tenant_s, held_s, q_ref, ent_ref,
                   part, pair, mine, landed, total, low_t, turned, up, ent_send,
                   up_sem, pair_send, pair_recv, rs_send, rs_recv, ag_send, ag_recv, fw_send, fw_recv,
                   en_send, en_recv):
    row, me = lax.axis_index("row"), lax.axis_index("kv")
    peers = lax.axis_size("kv")
    chips = peers // 2
    chip, core = me // 2, me % 2
    partner = (row, 2 * chip + 1 - core)
    wide = w_ref.shape[1]
    heads, width = q_ref.shape[1], q_ref.shape[2]
    own = q_ref.shape[0] // peers
    cap = ent_ref.shape[0] // peers
    barrier = pltpu.get_barrier_semaphore()

    def greet(i, c):
        pl.semaphore_signal(barrier, inc=1, device_id=(row, (me + i) % peers), device_id_type=MESH)
        return c

    lax.fori_loop(1, peers, greet, 0)
    up_copy = pltpu.make_async_copy(up_hbm, up, up_sem)
    up_copy.start()

    ht = ht_ref[...]
    part[:, :wide] = lax.dot_general(ht, w_ref[...], TN, preferred_element_type=F32)
    low = lax.dot_general(ht, dt_ref[...], TT, preferred_element_type=F32)
    rows, ranks = low.shape
    rank = ranks // 32
    is_tenant = jnp.where(tenant_ref[...] == iota((held_ref.shape[1], rows), 0), 1.0, 0.0).astype(BF16)
    held = jnp.broadcast_to(held_ref[...].astype(F32), (16, held_ref.shape[1])).astype(BF16)
    adapter = jnp.dot(held, is_tenant, preferred_element_type=F32)[0:8]
    adapter = jnp.transpose(adapter)[:, 0:1].astype(I32)
    low = jnp.where(lax.div(iota(low.shape, 1), rank) == adapter, low, 0.0)
    part[:, wide:] = sum(low[:, 128 * i: 128 * (i + 1)] for i in range(ranks // 128))

    dest, index, used = flat_row(holder_ref[...]), flat_row(index_ref[...]), flat_row(used_ref[...])
    count = dest.shape[1]
    to = dest == iota((peers, count), 0).astype(F32)
    earlier = jnp.where(iota((count, count), 0) < iota((count, count), 1), 1.0, 0.0).astype(BF16)
    before = jnp.dot(jnp.where(to, 1.0, 0.0).astype(BF16), earlier, preferred_element_type=F32)
    place = dest * cap + jnp.sum(jnp.where(to, before, 0.0), axis=0, keepdims=True)
    chosen = jnp.where(place == iota((peers * cap, count), 0).astype(F32), 1.0, 0.0).astype(BF16)
    sub = iota((128, count), 0)
    from_row = (me * own + lax.div(iota((1, count), 1), count // own)).astype(F32)
    fields = jnp.where(sub == 0, index, jnp.where(sub == 1, used, jnp.where(sub == 2, from_row, 0.0)))
    ent = lax.dot_general(chosen, fields.astype(BF16), NT, preferred_element_type=F32).astype(BF16)
    ent_send[...] = ent

    pl.semaphore_wait(barrier, peers - 1)

    def pair_copy(d):
        return remote(part.at[pl.ds((2 * d + 1 - core) * own, own)], pair.at[d],
                      pair_send.at[d], pair_recv.at[d], partner)

    def rs_copy(d, slot):
        return remote(mine.at[d], landed.at[slot], rs_send.at[d], rs_recv.at[slot], (row, 2 * d + core))

    def ent_copy(t, slot):
        return remote(ent_send.at[pl.ds(t * cap, cap)], ent_ref.at[pl.ds(slot * cap, cap)],
                      en_send.at[t], en_recv.at[slot], (row, t))

    def pair_start(i, c):
        pair_copy((chip + 1 + i) % chips).start()
        return c

    lax.fori_loop(0, chips, pair_start, 0)

    def forward(i, c):
        d = (chip + 1 + i) % chips
        pair_copy(d).wait_recv()
        mine[d] = part[pl.ds((2 * d + core) * own, own), :] + pair[d]
        rs_copy(d, chip).start()
        return c

    lax.fori_loop(0, chips - 1, forward, 0)
    pair_copy(chip).wait_recv()
    total[...] = part[pl.ds(me * own, own), :] + pair[chip]

    def ent_start(i, c):
        ent_copy((me + i) % peers, me).start()
        return c

    lax.fori_loop(1, peers, ent_start, 0)
    at = pl.ds(me * cap, cap)
    ent_ref[at, :] = ent_send[at, :]

    angles = (jnp.sum(used_ref[...], axis=1, keepdims=True) - 1).astype(F32) * freq_ref[...]
    cosine, sine = jnp.cos(angles), jnp.sin(angles)
    sine = jnp.where(iota(sine.shape, 1) < width // 2, -sine, sine)
    up_copy.wait()

    def gather(i, c):
        s = (chip + chips - 1 - i) % chips
        rs_copy(s, s).wait_recv()
        total[...] += landed[s]
        return c

    lax.fori_loop(0, chips - 1, gather, 0)

    low_t[...] = jnp.transpose(jnp.concatenate([total[:, wide:], jnp.zeros((128 - own, 128), F32)], axis=0)).reshape(low_t.shape)
    for r in range(own):
        adapter = held_s[tenant_s[me * own + r]]
        column = low_t[lax.rem(adapter, 128 // rank)][:, r:r + 1]
        more = jnp.sum(column * up[adapter], axis=0, keepdims=True)
        total[r:r + 1, :wide] += ADAPTER_SCALE * more
    gain = gain_ref[...]
    for h in range(heads):
        x = total[:, h * width:(h + 1) * width]
        x = x * lax.rsqrt(jnp.mean(x * x, axis=1, keepdims=True) + EPSILON) * gain
        turned[:, h, :] = x * cosine + pltpu.roll(x, width // 2, 1) * sine
    q_ref[pl.ds(me * own, own)] = turned[...].astype(BF16)

    def q_copy(d, owner, send, recv, device):
        at = pl.ds(owner * own, own)
        return remote(q_ref.at[at], q_ref.at[at], send, recv, device)

    def ag_copy(d, owner, slot):
        return q_copy(d, owner, ag_send.at[d], ag_recv.at[slot], (row, 2 * d + core))

    def fw_copy(d, owner):
        return q_copy(d, owner, fw_send.at[d], fw_recv.at[d], partner)

    def ag_start(i, c):
        ag_copy((chip + 1 + i) % chips, me, chip).start()
        return c

    lax.fori_loop(0, chips - 1, ag_start, 0)
    fw_copy(chip, me).start()

    def ag_forward(i, c):
        s = (chip + chips - 1 - i) % chips
        ag_copy(s, 2 * s + core, s).wait_recv()
        fw_copy(s, 2 * s + core).start()
        return c

    lax.fori_loop(0, chips - 1, ag_forward, 0)

    def finish(d, c):
        pair_copy(d).wait_send()
        fw_copy(d, 2 * d + 1 - core).wait_recv()
        fw_copy(d, 2 * d + core).wait_send()
        return c

    lax.fori_loop(0, chips, finish, 0)

    def finish_others(i, c):
        d = (chip + 1 + i) % chips
        rs_copy(d, chip).wait_send()
        ag_copy(d, me, chip).wait_send()
        return c

    lax.fori_loop(0, chips - 1, finish_others, 0)

    def finish_ent(i, c):
        t = (me + i) % peers
        ent_copy(t, t).wait_recv()
        ent_copy(t, me).wait_send()
        return c

    lax.fori_loop(1, peers, finish_ent, 0)


def project(ht, w, dt, up, gain, freq, holder, index, used, tenant, held, peers):
    rows, wide, width = ht.shape[1], w.shape[1], gain.shape[1]
    own = rows // peers
    cap = 2 * own * holder.shape[1] // peers
    chips = peers // 2
    heads = wide // width
    span = wide + 128
    vm = pl.BlockSpec(memory_space=pltpu.VMEM)
    sm = pl.BlockSpec(memory_space=pltpu.SMEM)
    dma = pltpu.SemaphoreType.DMA
    return pl.pallas_call(
        project_kernel,
        out_shape=[jax.ShapeDtypeStruct((rows, heads, width), BF16),
                   jax.ShapeDtypeStruct((peers * cap, 128), BF16)],
        in_specs=[vm, vm, vm, pl.BlockSpec(memory_space=pl.ANY), vm, vm, vm, vm, vm, vm, vm, sm, sm],
        out_specs=[vm, vm],
        scratch_shapes=[
            pltpu.VMEM((rows, span), F32), pltpu.VMEM((chips, own, span), F32),
            pltpu.VMEM((chips, own, span), F32), pltpu.VMEM((chips, own, span), F32),
            pltpu.VMEM((own, span), F32), pltpu.VMEM((128 // up.shape[1], up.shape[1], 128), F32),
            pltpu.VMEM((own, heads, width), F32),
            pltpu.VMEM(up.shape, F32), pltpu.VMEM((peers * cap, 128), BF16),
            dma, dma((chips,)), dma((chips,)), dma((chips,)), dma((chips,)), dma((chips,)), dma((chips,)),
            dma((chips,)), dma((chips,)), dma((peers,)), dma((peers,)),
        ],
        compiler_params=pltpu.CompilerParams(
            vmem_limit_bytes=40 * 2**20, collective_id=0, has_side_effects=True),
        name="project",
    )(ht, w, dt, up, gain, freq, holder, index, used, tenant.reshape(1, -1), held.reshape(1, -1), tenant, held)


def combine_kernel(p_ref, ml_ref, wo_ref, out_ref, parts, tops, flat, attended, terms, summed,
                   p_send, p_recv, m_send, m_recv, ag_send, ag_recv, fw_send, fw_recv, z_send, z_recv):
    row, me = lax.axis_index("row"), lax.axis_index("kv")
    peers, planes = lax.axis_size("kv"), lax.axis_size("row")
    chips = peers // 2
    chip, core = me // 2, me % 2
    partner = (row, 2 * chip + 1 - core)
    pair_rows = 16
    heads, width = p_ref.shape[2] // pair_rows, p_ref.shape[3]
    out_rows = out_ref.shape[0]
    barrier = pltpu.get_barrier_semaphore()

    def greet(i, c):
        pl.semaphore_signal(barrier, inc=1, device_id=(row, (me + i) % peers), device_id_type=MESH)
        return c

    def greet_plane(i, c):
        pl.semaphore_signal(barrier, inc=1, device_id=((row + i) % planes, me), device_id_type=MESH)
        return c

    lax.fori_loop(1, peers, greet, 0)
    lax.fori_loop(1, planes, greet_plane, 0)
    pl.semaphore_wait(barrier, peers + planes - 2)

    def part_copies(t, slot):
        return (remote(p_ref.at[t % 2, t // 2], parts.at[slot], p_send.at[t], p_recv.at[slot], (row, t)),
                remote(ml_ref.at[t % 2, t // 2], tops.at[slot], m_send.at[t], m_recv.at[slot], (row, t)))

    def part_start(i, c):
        for copy in part_copies((me + i) % peers, me):
            copy.start()
        return c

    lax.fori_loop(1, peers, part_start, 0)
    parts[me] = p_ref[core, chip]
    tops[me] = ml_ref[core, chip]

    def part_wait(i, c):
        t = (me + peers - i) % peers
        for copy in part_copies(t, t):
            copy.wait_recv()
        return c

    lax.fori_loop(1, peers, part_wait, 0)
    top, weight = tops[:, 0, :], tops[:, 1, :]
    factor = jnp.exp2(top - jnp.max(top, axis=0, keepdims=True))
    factor = factor / jnp.sum(factor * weight, axis=0, keepdims=True)
    factor = jnp.transpose(jnp.concatenate([factor, jnp.zeros((128 - peers, 128), F32)], axis=0))
    total = jnp.zeros((128, width), F32)
    for s in range(peers):
        total += factor[:, s:s + 1] * parts[s].astype(F32)
    flat[...] = total
    here = pl.ds(chip * pair_rows, pair_rows)
    for h in range(heads):
        attended[core, here, h * width:(h + 1) * width] = flat[pl.ds(h, pair_rows, stride=heads), :].astype(BF16)

    def at_copy(c, d, send, recv, device):
        at = pl.ds(d * pair_rows, pair_rows)
        return remote(attended.at[c, at], attended.at[c, at], send, recv, device)

    def ag_copy(d, source):
        return at_copy(core, source, ag_send.at[d], ag_recv.at[source], (row, 2 * d + core))

    def fw_copy(c, d):
        return at_copy(c, d, fw_send.at[d], fw_recv.at[d], partner)

    def ag_start(i, c):
        ag_copy((chip + 1 + i) % chips, chip).start()
        return c

    lax.fori_loop(0, chips - 1, ag_start, 0)
    fw_copy(core, chip).start()

    def ag_forward(i, c):
        s = (chip + chips - 1 - i) % chips
        ag_copy(s, s).wait_recv()
        fw_copy(core, s).start()
        return c

    lax.fori_loop(0, chips - 1, ag_forward, 0)

    def fw_wait(d, c):
        fw_copy(1 - core, d).wait_recv()
        return c

    lax.fori_loop(0, chips, fw_wait, 0)
    half = heads * width
    terms[...] = (lax.dot_general(attended[0], wo_ref[:, :half], NT, preferred_element_type=F32)
                  + lax.dot_general(attended[1], wo_ref[:, half:], NT, preferred_element_type=F32))

    def z_copy(z, slot):
        return remote(terms.at[pl.ds(z * out_rows, out_rows)], summed.at[slot], z_send.at[z], z_recv.at[slot], (z, me))

    for i in range(1, planes):
        z_copy((row + i) % planes, row).start()
    total = terms[pl.ds(row * out_rows, out_rows), :]
    for i in range(1, planes):
        z = (row + i) % planes
        z_copy(z, z).wait_recv()
        total += summed[z]
    out_ref[...] = total.astype(BF16)

    def finish(i, c):
        for copy in part_copies((me + i) % peers, me):
            copy.wait_send()
        return c

    lax.fori_loop(1, peers, finish, 0)

    def finish_ag(i, c):
        ag_copy((chip + 1 + i) % chips, chip).wait_send()
        return c

    lax.fori_loop(0, chips - 1, finish_ag, 0)

    def finish_fw(d, c):
        fw_copy(core, d).wait_send()
        return c

    lax.fori_loop(0, chips, finish_fw, 0)
    for i in range(1, planes):
        z_copy((row + i) % planes, row).wait_send()


def combine(p, ml, wo, peers, planes):
    chips = peers // 2
    rows = chips * 16
    wide = wo.shape[1]
    cols = wo.shape[0]
    vm = pl.BlockSpec(memory_space=pltpu.VMEM)
    dma = pltpu.SemaphoreType.DMA
    return pl.pallas_call(
        combine_kernel,
        out_shape=jax.ShapeDtypeStruct((rows // planes, cols), BF16),
        in_specs=[vm, vm, vm],
        out_specs=vm,
        scratch_shapes=[
            pltpu.VMEM((peers, 128, 128), BF16), pltpu.VMEM((peers, 8, 128), F32), pltpu.VMEM((128, 128), F32),
            pltpu.VMEM((2, rows, wide // 2), BF16), pltpu.VMEM((rows, cols), F32),
            pltpu.VMEM((planes, rows // planes, cols), F32),
            dma((peers,)), dma((peers,)), dma((peers,)), dma((peers,)),
            dma((chips,)), dma((chips,)), dma((chips,)), dma((chips,)), dma((planes,)), dma((planes,)),
        ],
        compiler_params=pltpu.CompilerParams(
            vmem_limit_bytes=40 * 2**20, collective_id=1, has_side_effects=True),
        name="combine",
    )(p, ml, wo)


def attend_kernel(group, unroll, q_ref, ent_ref, k_hbm, v_hbm, p_ref, ml_ref,
                  kbuf, vbuf, o_st, m_st, l_st, acc, mx, tot, tab_v, ent_v, tab, ent_s,
                  k_sem, v_sem, t_sem):
    blocks, toks, width = kbuf.shape
    rows, heads = q_ref.shape[0], q_ref.shape[1]
    slots = ent_ref.shape[0]
    owners = rows // 8
    per_owner = slots // owners
    positions = tab.shape[1]
    step = blocks // PIECES
    coef = math.log2(math.e) / math.sqrt(width)

    def piece(i):
        at = pl.ds(i * step, step)
        return (pltpu.make_async_copy(k_hbm.at[at], kbuf.at[at], k_sem.at[i]),
                pltpu.make_async_copy(v_hbm.at[at], vbuf.at[at], v_sem.at[i]))

    for i in range(PIECES):
        for copy in piece(i):
            copy.start()

    ent = ent_ref[...]
    entf = ent.astype(F32)
    pick = (lax.broadcasted_iota(I32, (16, 128), 0) == lax.broadcasted_iota(I32, (16, 128), 1)).astype(F32).astype(BF16)
    ent_t = lax.dot_general(pick, ent, NT, preferred_element_type=F32)
    blk_r, len_r, row_r = ent_t[0:1], ent_t[1:2], ent_t[2:3]
    key_c = jnp.where(entf[:, 1:2] > 0, entf[:, 0:1], 999.0)
    key_r = jnp.where(len_r > 0, blk_r, 999.0)
    earlier = lax.broadcasted_iota(I32, (slots, slots), 1) < lax.broadcasted_iota(I32, (slots, slots), 0)
    within = jnp.sum(jnp.where((key_c == key_r) & earlier, 1.0, 0.0), axis=1, keepdims=True)
    block_of = lax.broadcasted_iota(I32, (blocks, slots), 0).astype(F32) == key_r
    count = jnp.sum(jnp.where(block_of, 1.0, 0.0), axis=1, keepdims=True)
    chunks = jnp.floor((count + (group - 1)) * (1.0 / group))
    below = (lax.broadcasted_iota(I32, (blocks, blocks), 1) < lax.broadcasted_iota(I32, (blocks, blocks), 0))
    first = jnp.dot(jnp.where(below, 1.0, 0.0).astype(BF16),
                    jnp.broadcast_to(chunks, (blocks, 128)).astype(BF16), preferred_element_type=F32)
    total = jnp.sum(chunks, axis=0, keepdims=True)
    own_block = (key_c == lax.broadcasted_iota(I32, (slots, blocks), 1).astype(F32))
    first_c = jnp.dot(jnp.where(own_block, 1.0, 0.0).astype(BF16), first.astype(BF16),
                      preferred_element_type=F32)[:, 0:1]
    major = jnp.floor(within * (1.0 / group))
    place = (first_c + major) * group + (within - major * group)
    place = jnp.where(entf[:, 1:2] > 0, place, -1.0)
    slot_r = lax.broadcasted_iota(I32, (1, slots), 1) + 1
    half = lax.div(slot_r, 2)
    odd = slot_r - 2 * half
    sub = lax.broadcasted_iota(I32, (16, slots), 0)
    fields = jnp.where(sub == 0, blk_r, jnp.where(sub == 1, len_r, jnp.where(sub == 2, row_r, jnp.where(
        sub == 3, half.astype(F32), jnp.where(sub == 4, odd.astype(F32), 0.0))))).astype(BF16)
    chosen = jnp.where(place == lax.broadcasted_iota(I32, (slots, positions), 1).astype(F32), 1.0, 0.0).astype(BF16)
    table = jnp.dot(fields, chosen, preferred_element_type=F32)
    sub = lax.broadcasted_iota(I32, (8, positions), 0)
    t8 = table[0:8]
    tab_v[...] = jnp.where(sub == 1, 2.0 * t8, jnp.where(
        sub == 3, 2.0 * t8 + table[4:5], jnp.where(sub == 4, total, t8))).astype(I32)
    sub = lax.broadcasted_iota(I32, (8, slots), 0)
    last_row = (lax.div(lax.broadcasted_iota(I32, (1, slots), 1), per_owner) * 8 + 7).astype(F32)
    ent_v[...] = jnp.where(sub == 2, jnp.where(len_r > 0, row_r, last_row), ent_t[0:8]).astype(I32)
    copies = (pltpu.make_async_copy(tab_v, tab, t_sem.at[0]), pltpu.make_async_copy(ent_v, ent_s, t_sem.at[1]))
    for copy in copies:
        copy.start()
    acc[...] = jnp.zeros_like(acc)
    mx[...] = jnp.full_like(mx, NEG)
    tot[...] = jnp.zeros_like(tot)
    for copy in copies:
        copy.wait()

    col = lax.broadcasted_iota(I32, (heads, toks), 1)
    head = lax.broadcasted_iota(I32, (heads, toks), 0)
    match = (col & 1) == lax.div(head, heads // 2)
    col = jnp.where(match, col, 1 << 20)
    total_chunks = tab[4, 0]

    def chunk(c):
        base = c * group
        b = tab[0, base]
        q = jnp.concatenate([q_ref[tab[2, base + g]] for g in range(group)], axis=0)
        s = lax.dot_general(q, kbuf[b], NT, preferred_element_type=F32)
        s = jnp.concatenate(
            [jnp.where(col < tab[1, base + g], s[heads * g: heads * (g + 1)], NEG) for g in range(group)], axis=0)
        m = jnp.max(s, axis=1, keepdims=True)
        w = jnp.exp2((s - m) * coef)
        l = jnp.sum(w, axis=1, keepdims=True)
        o = jnp.dot(w.astype(BF16), vbuf[b], preferred_element_type=F32)
        return o, m, l

    def store(c, res):
        o, m, l = res
        for g in range(group):
            slot = tab[3, c * group + g]
            at = slice(heads * g, heads * (g + 1))
            o_st[slot] = o[at]
            m_st[slot] = jnp.broadcast_to(m[at] * coef, (heads, width))
            l_st[slot] = jnp.broadcast_to(l[at], (heads, width))

    def wait_piece(i, carry):
        for copy in piece(i):
            copy.wait()
        return carry

    def body(i, waited):
        c = i * unroll
        need = 0
        for u in range(unroll):
            need = jnp.maximum(need, tab[0, (c + u) * group])
        need = lax.div(need, step) + 1
        lax.fori_loop(waited, need, wait_piece, 0)
        waited = jnp.maximum(waited, need)
        res = [chunk(c + u) for u in range(unroll)]
        for u in range(unroll):
            store(c + u, res[u])
        return waited

    waited = lax.fori_loop(0, lax.div(total_chunks + unroll - 1, unroll), body, 0)
    lax.fori_loop(waited, PIECES, wait_piece, 0)

    def merge(o, carry):
        m = jnp.full((heads, width), NEG, F32)
        a = jnp.zeros((heads, width), F32)
        l = a
        prev = -1
        for p in range(per_owner):
            slot = o * per_owner + p
            row = ent_s[2, slot]
            valid = ent_s[1, slot] > 0
            mp = jnp.where(valid, m_st[slot + 1], NEG)
            lp = jnp.where(valid, l_st[slot + 1], 0.0)
            op = jnp.where(valid, o_st[slot + 1], 0.0)
            mo = jnp.where(row == prev, m, NEG)
            m = jnp.maximum(mo, mp)
            fa = jnp.exp2(mo - m)
            fb = jnp.exp2(mp - m)
            a = fa * a + fb * op
            l = fa * l + fb * lp
            acc[row] = a
            mx[row] = m
            tot[row] = l
            prev = row
        return carry

    lax.fori_loop(0, owners, merge, 0)

    eye = lax.broadcasted_iota(I32, (128, 128), 0) == lax.broadcasted_iota(I32, (128, 128), 1)

    def finish(d, carry):
        at = pl.ds(d * 16, 16)
        for c in range(2):
            hs = slice(8 * c, 8 * c + 8)
            p_ref[c, d] = acc[at, hs, :].reshape(128, width).astype(BF16)
            m = jnp.sum(jnp.where(eye, mx[at, hs, :].reshape(128, width), 0.0), axis=0, keepdims=True)
            l = jnp.sum(jnp.where(eye, tot[at, hs, :].reshape(128, width), 0.0), axis=0, keepdims=True)
            ml_ref[c, d] = jnp.where(lax.broadcasted_iota(I32, (8, 128), 0) == 0, m, l)
        return carry

    lax.fori_loop(0, rows // 16, finish, 0)


def attend(q, ent, k, v, group=8, unroll=16):
    rows, heads, width = q.shape
    blocks, toks, _ = k.shape
    slots = ent.shape[0]
    nc = slots // group + blocks * (group - 1) // group
    nc = -(-nc // unroll) * unroll
    positions = -(-nc * group // 128) * 128
    vm = pl.BlockSpec(memory_space=pltpu.VMEM)
    return pl.pallas_call(
        functools.partial(attend_kernel, group, unroll),
        out_shape=[jax.ShapeDtypeStruct((2, rows // 16, 128, width), BF16),
                   jax.ShapeDtypeStruct((2, rows // 16, 8, 128), F32)],
        in_specs=[vm, vm, pl.BlockSpec(memory_space=pl.ANY), pl.BlockSpec(memory_space=pl.ANY)],
        out_specs=[vm, vm],
        scratch_shapes=[
            pltpu.VMEM((blocks, toks, width), BF16), pltpu.VMEM((blocks, toks, width), BF16),
            pltpu.VMEM((slots + 1, heads, width), F32), pltpu.VMEM((slots + 1, heads, width), F32),
            pltpu.VMEM((slots + 1, heads, width), F32),
            pltpu.VMEM((rows, heads, width), F32), pltpu.VMEM((rows, heads, width), F32),
            pltpu.VMEM((rows, heads, width), F32),
            pltpu.VMEM((8, positions), I32), pltpu.VMEM((8, slots), I32),
            pltpu.SMEM((8, positions), I32), pltpu.SMEM((8, slots), I32),
            pltpu.SemaphoreType.DMA((PIECES,)), pltpu.SemaphoreType.DMA((PIECES,)), pltpu.SemaphoreType.DMA((2,)),
        ],
        compiler_params=pltpu.CompilerParams(vmem_limit_bytes=56 * 2**20),
        name="attend",
    )(q, ent, k, v)


def local(hidden, query_weight, adapter_down_weight, adapter_up_weight, query_norm_gain, paged_key_cache,
          paged_value_cache, output_weight, holder, holder_block_index, block_used_length, tenant, tenant_adapter):
    peers, planes = lax.axis_size("kv"), lax.axis_size("row")
    count, _, rank = adapter_down_weight.shape
    width = query_norm_gain.shape[0]
    blocks, toks, kv_heads, _ = paged_key_cache.shape
    half = width // 2
    freq = ROPE_BASE ** (-(jnp.arange(half, dtype=jnp.float32) * 2.0) / width)
    freq = jnp.concatenate([freq, freq])[None, :]
    down = jnp.transpose(adapter_down_weight, (0, 2, 1)).reshape(count * rank, -1)
    q, ent = project(hidden.T, query_weight, down, adapter_up_weight, query_norm_gain[None, :], freq, holder, holder_block_index,
                     block_used_length, tenant, tenant_adapter, peers)
    p, ml = attend(q, ent, paged_key_cache.reshape(blocks, toks * kv_heads, width),
                   paged_value_cache.reshape(blocks, toks * kv_heads, width))
    return combine(p, ml, output_weight.T, peers, planes)


def solution(mesh):
    return jax.shard_map(
        local,
        mesh=mesh,
        in_specs=(
            P(None, "kv"),
            P("kv", "row"),
            P(None, "kv", None),
            P(None, None, "row"),
            P(),
            P("kv", None, "row", None),
            P("kv", None, "row", None),
            P("row", "kv"),
            P("kv", None),
            P("kv", None),
            P("kv", None),
            P(),
            P(),
        ),
        out_specs=P("row", "kv"),
        check_vma=False,
    )
```

time: 572 us -> 123 us (0.22)
  matrix products: 176 us -> 0 us
  blocking collectives: 123 us -> 0 us
  waiting for transfers between devices: 120 us -> 0 us
  Pallas kernels: 0 us -> 109 us
  local copies, waits for them, and re-layouts: 74.1 us -> 13.5 us
  starting transfers between devices: 37.5 us -> 0 us
  other arithmetic: 20.6 us -> 0.09 us
  between operations: 14.4 us -> 0.06 us
    dot_general x12 -> x0, matrix products: 176 us -> none  [the longest x1 85.2 us: local(): jnp.einsum('rajd,rtad->rajt', grouped, keys, preferred_element_type=jnp.f...]
    unnamed x1 -> x0, blocking collectives: 123 us -> none
    pallas_call x0 -> x3, Pallas kernels: none -> 109 us  [the longest x1 44.8 us: combine(): pl.pallas_call(combine_kernel, out_shape=jax.ShapeDtypeStruct((rows // pl...]
    all_to_all x5 -> x0, waiting for transfers between devices: 57.7 us -> none  [the longest x1 46.4 us: local(): lax.all_to_all(block_out, 'kv', split_axis=0, concat_axis=0, tiled=True)]
    all_gather x1 -> x0, waiting for transfers between devices: 45.1 us -> none  [local(): lax.all_gather(attention, 'kv', axis=0, tiled=True)]
    reshape x11 -> x0, local copies, waits for them, and re-layouts: 40.7 us -> none  [the longest x1 14.4 us: local(): paged_key_cache.reshape(local_blocks, block_size * kv_local * head_size)]
    all_to_all x5 -> x0, starting transfers between devices: 37.2 us -> none  [the longest x1 9.32 us: local(): lax.all_to_all(sent_queries, 'kv', split_axis=0, concat_axis=0, tiled=True)]
    dot_general x3 -> x0, local copies, waits for them, and re-layouts: 24 us -> none  [the longest x1 11.9 us: local(): jnp.dot(block_pick, flat_values, preferred_element_type=jnp.bfloat16)]
  transfers between devices with their start and end apart: 8 -> 0, of which waited for: 4 -> 0; matrix products, arithmetic and copies ran while one was open for 24% -> 0% of each run, Pallas kernels for 0% -> 0%
where the time goes in v1:
time: 123 us
  Pallas kernels  109 us (89%)
  local copies, waits for them, and re-layouts  13.5 us (11%)
    pallas_call x1, Pallas kernels, combine(): pl.pallas_call(combine_kernel, out_shape=jax.ShapeDtypeStruct((rows // pl...  44.8 us
    pallas_call x1, Pallas kernels, project(): pl.pallas_call(project_kernel, out_shape=[jax.ShapeDtypeStruct((rows, hea...  43 us
    pallas_call x1, Pallas kernels, attend(): pl.pallas_call(functools.partial(attend_kernel, group, unroll), out_shape...  21.5 us
    unnamed x31, local copies, waits for them, and re-layouts  13.5 us

profile of v1, /device:TPU:1, one launch (start us, length us, event | category | flops | bytes accessed | tf_op | source)
XLA Modules:
  0.0 122.9 jit_solution(9555242376296189719)
XLA Ops:
  0.0 0.1 maximum_bitcast_fusion.freq_ref
  0.1 0.0 copy-start
  0.1 2.2 %copy-done = f32[32,16,2048]{2,1,0:T(8,128)S(1)} copy-done((f32[32,16,2048]{2,1,0:T(8,128)S(1)}, f32[32,16,2048]{2,1,0:T(8,128)}, u32[]{:S(2)}) %copy-start) | copy-done | bytes 4194328
  2.3 0.0 copy-start.3
  2.3 1.1 copy-done.3
  3.4 0.9 copy-done.5
  4.3 0.9 copy-done.8
  5.2 0.7 copy-done.9
  5.9 0.7 copy-done.10
  6.6 0.7 copy-done.11
  7.3 0.7 copy-done.12
  8.0 0.7 copy-done.13
  8.6 0.7 copy-done.14
  9.3 43.0 %project.1 = (bf16[256,16,128]{2,1,0:T(8,128)(2,1)S(1)}, bf16[512,128]{1,0:T(8,128)(2,1)S(1)}) custom-call(bf16[160,256]{1,0:T(8,128)(2,1)S(1)} %bitcast.14, bf16[160,2048]{1,0:T(8,128)(2,1)S(1)} %copy-done.3, bf16[512,160]{1,0:T(8,128)(2,1)S(1)} %bitcast.13, f32[32,16,2048]{2,1,0:T(8,128)S(1)} %copy-done, f32[1,128]{1,0:T(1,128)S(1)} %bitcast.17, ...), custom_call_target="tpu_custom_call" | custom-call | tf_op jit(solution)/shard_map/project/pallas_call | solution.py:212
  52.2 0.0 copy-start.1
  52.3 1.0 copy-done.1
  53.2 0.6 copy-done.6
  53.9 21.5 %attend.1 = (bf16[2,16,128,128]{3,2,1,0:T(8,128)(2,1)}, f32[2,16,8,128]{3,2,1,0:T(8,128)}) custom-call(bf16[256,16,128]{2,1,0:T(8,128)(2,1)} %copy-done.1, bf16[512,128]{1,0:T(8,128)(2,1)} %copy-done.6, bf16[128,256,128]{2,1,0:T(8,128)(2,1)} %bitcast.18, bf16[128,256,128]{2,1,0:T(8,128)(2,1)} %bitcast.19), custom_call_target="tpu_custom_call" | custom-call | tf_op jit(solution)/shard_map/attend/pallas_call | solution.py:547
  75.4 0.0 copy-done.4
  75.4 0.0 copy-start.2
  75.4 1.2 copy-done.2
  76.6 0.9 copy-done.7
  77.5 44.8 %combine.1 = bf16[64,160]{1,0:T(8,128)(2,1)S(1)} custom-call(bf16[2,16,128,128]{3,2,1,0:T(8,128)(2,1)S(1)} %copy-done.2, f32[2,16,8,128]{3,2,1,0:T(8,128)S(1)} %copy-done.7, bf16[160,2048]{1,0:T(8,128)(2,1)S(1)} %bitcast.12), custom_call_target="tpu_custom_call" | custom-call | tf_op jit(solution)/shard_map/combine/pallas_call | solution.py:364
  122.3 0.6 copy.15
  (12 shorter events, 0.0 us)
Async XLA Ops:
  0.1 2.2 %copy-start = (f32[32,16,2048]{2,1,0:T(8,128)S(1)}, f32[32,16,2048]{2,1,0:T(8,128)}, u32[]{:S(2)}) copy-start(f32[32,16,2048]{2,1,0:T(8,128)} %up_hbm.1) | copy-start | bytes 12582916
  2.3 1.1 copy-start.3
  3.4 0.9 copy-start.5
  4.3 0.9 copy-start.8
  5.2 0.7 copy-start.9
  5.9 0.7 copy-start.10
  6.6 0.7 copy-start.11
  7.3 0.7 copy-start.12
  8.0 0.7 copy-start.13
  8.6 0.7 copy-start.14
  52.2 1.0 copy-start.1
  53.2 0.7 copy-start.6
  53.9 21.5 %copy-start.4 = (bf16[2048,160]{0,1:T(8,128)(2,1)S(1)}, bf16[2048,160]{0,1:T(8,128)(2,1)}, u32[]{:S(2)}) copy-start(bf16[2048,160]{0,1:T(8,128)(2,1)} %param.20) | copy-start | bytes 1966084
  75.4 1.2 copy-start.2
  76.6 0.9 copy-start.7

commit v2 on v0

v2 whole, which is shorter than its diff:
```python
import functools
import math

import jax
import jax.numpy as jnp
from jax import lax
from jax.experimental import pallas as pl
from jax.experimental.pallas import tpu as pltpu
from jax.sharding import PartitionSpec as P

NEG = -1e30
F32, BF16, I32 = jnp.float32, jnp.bfloat16, jnp.int32
NT = (((1,), (1,)), ((), ()))
TN = (((0,), (0,)), ((), ()))
TT = (((0,), (1,)), ((), ()))
MESH = pl.DeviceIdType.MESH
PIECES = 4
GROUP = 8
UNROLL = 16
SIDE = 4
ADAPTER_SCALE = 0.5
ROPE_BASE = 1000000.0
EPSILON = 1e-06


def iota(shape, dim):
    return lax.broadcasted_iota(I32, shape, dim)


def flat_row(x):
    rows, n = x.shape
    wide = jnp.concatenate([x.astype(F32)] * rows, axis=1)
    keep = lax.div(iota(wide.shape, 1), n) == iota(wide.shape, 0)
    return jnp.sum(jnp.where(keep, wide, 0.0), axis=0, keepdims=True)


def remote(src, dst, send, recv, device):
    return pltpu.make_async_remote_copy(
        src_ref=src, dst_ref=dst, send_sem=send, recv_sem=recv, device_id=device, device_id_type=MESH)


def entries_by_holder(holder, index, used, me, own, peers, cap):
    dest, index, used = flat_row(holder), flat_row(index), flat_row(used)
    count = dest.shape[1]
    to = dest == iota((peers, count), 0).astype(F32)
    earlier = jnp.where(iota((count, count), 0) < iota((count, count), 1), 1.0, 0.0).astype(BF16)
    before = jnp.dot(jnp.where(to, 1.0, 0.0).astype(BF16), earlier, preferred_element_type=F32)
    place = dest * cap + jnp.sum(jnp.where(to, before, 0.0), axis=0, keepdims=True)
    chosen = jnp.where(place == iota((peers * cap, count), 0).astype(F32), 1.0, 0.0).astype(BF16)
    sub = iota((128, count), 0)
    from_row = (me * own + lax.div(iota((1, count), 1), count // own)).astype(F32)
    fields = jnp.where(sub == 0, index, jnp.where(sub == 1, used, jnp.where(sub == 2, from_row, 0.0)))
    return lax.dot_general(chosen, fields.astype(BF16), NT, preferred_element_type=F32).astype(BF16)


def order_entries(ent, blocks, rows, positions, per_group):
    slots = ent.shape[0]
    entf = ent.astype(F32)
    pick = jnp.where(iota((16, 128), 0) == iota((16, 128), 1), 1.0, 0.0).astype(BF16)
    ent_t = lax.dot_general(pick, ent, NT, preferred_element_type=F32)
    blk_r, len_r, row_r = ent_t[0:1], ent_t[1:2], ent_t[2:3]
    valid_c = entf[:, 1:2] > 0
    key_c = jnp.where(valid_c, entf[:, 0:1], 999.0)
    key_r = jnp.where(len_r > 0, blk_r, 999.0)
    earlier = iota((slots, slots), 1) < iota((slots, slots), 0)
    within = jnp.sum(jnp.where((key_c == key_r) & earlier, 1.0, 0.0), axis=1, keepdims=True)
    block_of = iota((blocks, slots), 0).astype(F32) == key_r
    count = jnp.sum(jnp.where(block_of, 1.0, 0.0), axis=1, keepdims=True)
    chunks = jnp.floor((count + (GROUP - 1)) * (1.0 / GROUP))
    below = jnp.where(iota((blocks, blocks), 1) < iota((blocks, blocks), 0), 1.0, 0.0).astype(BF16)
    first = jnp.dot(below, jnp.broadcast_to(chunks, (blocks, 128)).astype(BF16), preferred_element_type=F32)
    own_block = jnp.where(key_c == iota((slots, blocks), 1).astype(F32), 1.0, 0.0).astype(BF16)
    first_c = jnp.dot(own_block, first.astype(BF16), preferred_element_type=F32)[:, 0:1]
    major = jnp.floor(within * (1.0 / GROUP))
    chunk_c, seat_c = first_c + major, within - major * GROUP
    place = jnp.where(valid_c, chunk_c * GROUP + seat_c, -1.0)
    sub = iota((16, slots), 0)
    fields = jnp.where(sub == 0, blk_r, jnp.where(sub == 1, len_r, jnp.where(sub == 2, row_r, 0.0))).astype(BF16)
    chosen = jnp.where(place == iota((slots, positions), 1).astype(F32), 1.0, 0.0).astype(BF16)
    table = jnp.dot(fields, chosen, preferred_element_type=F32)[0:8]
    sub = iota(table.shape, 0)
    table = jnp.where(sub == 1, 2.0 * table, table).astype(I32)
    table = jnp.clip(table, 0, jnp.where(sub == 0, blocks - 1, jnp.where(sub == 1, 1 << 16, rows - 1)))
    lane = iota((slots, 128), 1)
    seats = jnp.where(lane == 0, chunk_c, jnp.where(lane == 1, seat_c, 0.0)).astype(BF16)
    seats = lax.dot_general(pick, seats, NT, preferred_element_type=F32)
    where_r = jnp.where(len_r > 0, seats[0:1] * GROUP + seats[1:2], 0.0)
    local_r = row_r - (lax.div(iota((1, slots), 1), per_group) * 16).astype(F32)
    local_r = jnp.where(len_r > 0, local_r, -1.0)
    by_slot = jnp.clip(jnp.where(iota((8, slots), 0) == 0, where_r, local_r).astype(I32), -1, positions - 1)
    by_slot = jnp.where(iota((8, slots), 0) == 0, jnp.maximum(by_slot, 0), by_slot)
    return table, by_slot


def kernel(ht_h, w_h, dt_h, up_h, gain_h, freq_h, holder_h, index_h, used_h, tenant_h, held_h, k_h, v_h, wo_h,
           out_ref,
           ht, w, dt, up, gain, freq, holder, index, used, tenant, held, tenant_s, held_s, kbuf, vbuf, wo,
           part, pair, mine_a, mine_b, land_a, land_b, sum_a, sum_b, end_a, end_b, total, low_t, turned,
           ent_send, ent, tab_v, slot_v, tab, slot_s, q, o_st, e_st,
           partial, tops, partial_in, tops_in, merged, tops_out, parts, tops_all, flat, attended, terms, summed,
           in_sem, kv_sem, tab_sem, pair_send, pair_recv, a_send, a_recv, b_send, b_recv, a2_send, a2_recv,
           b2_send, b2_recv, en_send, en_recv, ag_send, ag_recv, fw_send, fw_recv,
           x_send, x_recv, p_send, p_recv, t_send, t_recv, ag2_send, ag2_recv, fw2_send, fw2_recv, z_send, z_recv):
    row, me = lax.axis_index("row"), lax.axis_index("kv")
    peers, planes = lax.axis_size("kv"), lax.axis_size("row")
    chips = peers // 2
    chip, core = me // 2, me % 2
    x, y = chip // SIDE, chip % SIDE
    partner = (row, 2 * chip + 1 - core)
    wide = w.shape[1]
    rows, heads, width = q.shape
    own = rows // peers
    cap = ent.shape[0] // peers
    blocks, toks, _ = kbuf.shape
    wide_a = mine_a.shape[3]
    barrier = pltpu.get_barrier_semaphore()

    def greet(i, c):
        pl.semaphore_signal(barrier, inc=1, device_id=(row, (me + i) % peers), device_id_type=MESH)
        return c

    def greet_plane(i, c):
        pl.semaphore_signal(barrier, inc=1, device_id=((row + i) % planes, me), device_id_type=MESH)
        return c

    lax.fori_loop(1, peers, greet, 0)
    lax.fori_loop(1, planes, greet_plane, 0)

    loads = [pltpu.make_async_copy(src, dst, in_sem.at[i]) for i, (src, dst) in enumerate((
        (ht_h, ht), (w_h, w), (holder_h, holder), (index_h, index), (used_h, used), (tenant_h, tenant),
        (held_h, held), (dt_h, dt), (tenant_h, tenant_s), (held_h, held_s), (gain_h, gain), (freq_h, freq),
        (up_h, up), (wo_h, wo)))]
    for copy in loads:
        copy.start()
    step = blocks // PIECES
    pool = []
    for i in range(PIECES):
        at = pl.ds(i * step, step)
        pool += [pltpu.make_async_copy(k_h.at[at], kbuf.at[at], kv_sem.at[2 * i]),
                 pltpu.make_async_copy(v_h.at[at], vbuf.at[at], kv_sem.at[2 * i + 1])]
    for copy in pool:
        copy.start()
    for copy in loads[:8]:
        copy.wait()

    part[:, :wide] = lax.dot_general(ht[...], w[...], TN, preferred_element_type=F32)
    low = lax.dot_general(ht[...], dt[...], TT, preferred_element_type=F32)
    rank = up.shape[1]
    is_tenant = jnp.where(tenant[...] == iota((held.shape[1], rows), 0), 1.0, 0.0).astype(BF16)
    held_b = jnp.broadcast_to(held[...].astype(F32), (16, held.shape[1])).astype(BF16)
    adapter = jnp.dot(held_b, is_tenant, preferred_element_type=F32)[0:8]
    adapter = jnp.transpose(adapter)[:, 0:1].astype(I32)
    low = jnp.where(lax.div(iota(low.shape, 1), rank) == adapter, low, 0.0)
    part[:, wide:] = sum(low[:, 128 * i: 128 * (i + 1)] for i in range(low.shape[1] // 128))
    ent_send[...] = entries_by_holder(holder[...], index[...], used[...], me, own, peers, cap)

    pl.semaphore_wait(barrier, peers + planes - 2)

    def pair_copy(d):
        return remote(part.at[pl.ds((2 * d + 1 - core) * own, own)], pair.at[d],
                      pair_send.at[d], pair_recv.at[d], partner)

    def chip_at(ox, oy):
        return (x + ox) % SIDE, (y + oy) % SIDE

    hops = (2, 1, 3, 0)
    for ox in hops:
        for oy in hops:
            dx, dy = chip_at(ox, oy)
            pair_copy(dx * SIDE + dy).start()

    def a_copy(t, s):
        return remote(mine_a.at[t], land_a.at[s], a_send.at[t], a_recv.at[s], (row, 2 * (t * SIDE + y) + core))

    def b_copy(t, i, s):
        return remote(mine_b.at[t, i], land_b.at[s, i], b_send.at[t, i], b_recv.at[s, i],
                      (row, 2 * (x * SIDE + t) + core))

    for ox in hops:
        for oy in hops:
            dx, dy = chip_at(ox, oy)
            d = dx * SIDE + dy
            pair_copy(d).wait_recv()
            both = part[pl.ds((2 * d + core) * own, own), :] + pair[d]
            mine_a[dx, dy] = both[:, :wide_a]
            mine_b[dy, dx] = both[:, wide_a:]
            if oy:
                b_copy(dy, dx, y).start()
        if ox:
            a_copy(dx, x).start()

    def ent_copy(t, slot):
        return remote(ent_send.at[pl.ds(t * cap, cap)], ent.at[pl.ds(slot * cap, cap)],
                      en_send.at[t], en_recv.at[slot], (row, t))

    def ent_start(i, c):
        ent_copy((me + i) % peers, me).start()
        return c

    lax.fori_loop(1, peers, ent_start, 0)
    at = pl.ds(me * cap, cap)
    ent[at, :] = ent_send[at, :]
    for copy in loads[8:]:
        copy.wait()
    angles = (jnp.sum(used[...], axis=1, keepdims=True) - 1).astype(F32) * freq[...]
    cosine, sine = jnp.cos(angles), jnp.sin(angles)
    sine = jnp.where(iota(sine.shape, 1) < width // 2, -sine, sine)

    def a2_copy(t, s):
        return remote(sum_a.at[t], end_a.at[s], a2_send.at[t], a2_recv.at[s], (row, 2 * (x * SIDE + t) + core))

    def b2_copy(t, s):
        return remote(sum_b.at[t], end_b.at[s], b2_send.at[t], b2_recv.at[s], (row, 2 * (t * SIDE + y) + core))

    steps = (1, 3, 2)
    for o in steps:
        a_copy((x + SIDE - o) % SIDE, (x + SIDE - o) % SIDE).wait_recv()
    sum_a[...] = mine_a[x] + land_a[(x + 1) % SIDE] + land_a[(x + 2) % SIDE] + land_a[(x + 3) % SIDE]
    for o in (2, 1, 3):
        a2_copy((y + o) % SIDE, y).start()
    for o in steps:
        for i in range(SIDE):
            b_copy((y + SIDE - o) % SIDE, i, (y + SIDE - o) % SIDE).wait_recv()
    sum_b[...] = mine_b[y] + land_b[(y + 1) % SIDE] + land_b[(y + 2) % SIDE] + land_b[(y + 3) % SIDE]
    for o in (2, 1, 3):
        b2_copy((x + o) % SIDE, x).start()

    def ent_wait(i, c):
        t = (me + peers - i) % peers
        ent_copy(t, t).wait_recv()
        return c

    lax.fori_loop(1, peers, ent_wait, 0)
    table, by_slot = order_entries(ent[...], blocks, rows, tab.shape[1], 2 * cap)
    tab_v[...] = table
    slot_v[...] = by_slot
    tables = (pltpu.make_async_copy(tab_v, tab, tab_sem.at[0]), pltpu.make_async_copy(slot_v, slot_s, tab_sem.at[1]))
    for copy in tables:
        copy.start()

    for o in steps:
        a2_copy((y + SIDE - o) % SIDE, (y + SIDE - o) % SIDE).wait_recv()
    total[:, :wide_a] = sum_a[y] + end_a[(y + 1) % SIDE] + end_a[(y + 2) % SIDE] + end_a[(y + 3) % SIDE]
    for o in steps:
        b2_copy((x + SIDE - o) % SIDE, (x + SIDE - o) % SIDE).wait_recv()
    total[:, wide_a:] = sum_b[x] + end_b[(x + 1) % SIDE] + end_b[(x + 2) % SIDE] + end_b[(x + 3) % SIDE]

    low_t[...] = jnp.transpose(
        jnp.concatenate([total[:, wide:], jnp.zeros((128 - own, 128), F32)], axis=0)).reshape(low_t.shape)
    for r in range(own):
        adapter = held_s[0, tenant_s[0, me * own + r]]
        column = low_t[lax.rem(adapter, 128 // rank)][:, r:r + 1]
        more = jnp.sum(column * up[adapter], axis=0, keepdims=True)
        total[r:r + 1, :wide] += ADAPTER_SCALE * more
    gain_r = gain[...]
    for h in range(heads):
        t = total[:, h * width:(h + 1) * width]
        t = t * lax.rsqrt(jnp.mean(t * t, axis=1, keepdims=True) + EPSILON) * gain_r
        turned[:, h, :] = t * cosine + pltpu.roll(t, width // 2, 1) * sine
    q[pl.ds(me * own, own)] = turned[...].astype(BF16)

    def spread(copy_of, first_ref, relay_copy):
        def start(i, c):
            i = (5 * i) % chips
            copy_of(((x + i // SIDE) % SIDE) * SIDE + (y + i % SIDE) % SIDE, chip).start()
            return c

        def relay(i, c):
            i = (5 * i) % chips
            s = ((x + SIDE - i // SIDE) % SIDE) * SIDE + (y + SIDE - i % SIDE) % SIDE
            copy_of(s, s).wait_recv()
            relay_copy(s, core).start()
            return c

        def landed(d, c):
            relay_copy(d, 1 - core).wait_recv()
            return c

        lax.fori_loop(1, chips, start, 0)
        relay_copy(chip, core).start()
        lax.fori_loop(1, chips, relay, 0)
        lax.fori_loop(0, chips, landed, 0)

    def spread_end(copy_of, relay_copy):
        def sent(i, c):
            copy_of((chip + i) % chips, chip).wait_send()
            return c

        def relayed(d, c):
            relay_copy(d, core).wait_send()
            return c

        lax.fori_loop(1, chips, sent, 0)
        lax.fori_loop(0, chips, relayed, 0)

    def q_copy(d, s):
        at = pl.ds((2 * s + core) * own, own)
        return remote(q.at[at], q.at[at], ag_send.at[d], ag_recv.at[s], (row, 2 * d + core))

    def q_relay(s, c):
        at = pl.ds((2 * s + c) * own, own)
        return remote(q.at[at], q.at[at], fw_send.at[s], fw_recv.at[s], partner)

    spread(q_copy, None, q_relay)
    for copy in tables:
        copy.wait()
    for copy in pool:
        copy.wait()

    coef = math.log2(math.e) / math.sqrt(width)
    col = iota((heads, toks), 1)
    col = jnp.where((col & 1) == lax.div(iota((heads, toks), 0), heads // 2), col, 1 << 20)

    def chunk(c):
        base = c * GROUP
        b = tab[0, base]
        qs = jnp.concatenate([q[tab[2, base + g]] for g in range(GROUP)], axis=0)
        s = lax.dot_general(qs, kbuf[b], NT, preferred_element_type=F32)
        s = jnp.concatenate(
            [jnp.where(col < tab[1, base + g], s[heads * g: heads * (g + 1)], NEG) for g in range(GROUP)], axis=0)
        m = jnp.max(s, axis=1, keepdims=True)
        wt = jnp.exp2((s - m) * coef)
        l = jnp.sum(wt, axis=1, keepdims=True)
        o = jnp.dot(wt.astype(BF16), vbuf[b], preferred_element_type=F32) / l
        e = jnp.broadcast_to(m * coef + jnp.log2(l), o.shape)
        return o.reshape(GROUP, 2, heads // 2, width), e.reshape(GROUP, 2, heads // 2, width)

    def chunks(i, c):
        done = [chunk(i * UNROLL + u) for u in range(UNROLL)]
        for u in range(UNROLL):
            o, e = done[u]
            at = pl.ds((i * UNROLL + u) * GROUP, GROUP)
            o_st[at] = o
            e_st[at] = e
        return c

    lax.fori_loop(0, tab.shape[1] // (GROUP * UNROLL), chunks, 0)

    half = heads // 2
    lane = iota((half, 128), 1)
    same_head = (lane & (half - 1)) == iota((half, 128), 0)
    lane_row = jnp.where(same_head, lax.div(lane, half), -2)
    slots = 2 * cap

    def merge(d, c):
        for hv in range(2):
            tops_of, outs = [], []
            for p in range(slots):
                at = slot_s[0, d * slots + p]
                tops_of.append(jnp.where(lane_row == slot_s[1, d * slots + p], e_st[at, hv], NEG))
                outs.append(o_st[at, hv])
            es = jnp.concatenate(tops_of, axis=0)
            top = jnp.max(es, axis=0, keepdims=True)
            f = jnp.exp2(es - top)
            l = jnp.sum(f, axis=0, keepdims=True)
            f = (f * (1.0 / l)).astype(BF16)
            os = jnp.concatenate(outs, axis=0).astype(BF16)
            partial[hv, d] = lax.dot_general(f, os, TN, preferred_element_type=F32).astype(BF16)
            tops[hv, pl.ds(d, 1), :] = top + jnp.log2(l)
        return c

    lax.fori_loop(0, chips, merge, 0)

    x_copies = (remote(partial.at[1 - core], partial_in, x_send.at[0], x_recv.at[0], partner),
                remote(tops.at[1 - core], tops_in, x_send.at[1], x_recv.at[1], partner))
    for copy in x_copies[::-1]:
        copy.start()

    def columns(fs):
        n = fs.shape[0]
        return jnp.transpose(jnp.concatenate([fs, jnp.zeros((128 - n, 128), F32)], axis=0))

    x_copies[1].wait_recv()
    t0, t1 = tops[core], tops_in[...]
    top = jnp.maximum(t0, t1)
    f0, f1 = jnp.exp2(t0 - top), jnp.exp2(t1 - top)
    l = f0 + f1
    over = top + jnp.log2(l)
    for d in range(chips):
        tops_out[d] = jnp.broadcast_to(over[d:d + 1], (8, 128))
    f = columns(jnp.concatenate([f0 / l, f1 / l], axis=0))

    def t_copy(d, s):
        return remote(tops_out.at[d], tops_all.at[s], t_send.at[d], t_recv.at[s], (row, 2 * d + core))

    def p_copy(d, s):
        return remote(merged.at[d], parts.at[s], p_send.at[d], p_recv.at[s], (row, 2 * d + core))

    def t_start(i, c):
        i = (5 * i) % chips
        t_copy(((x + i // SIDE) % SIDE) * SIDE + (y + i % SIDE) % SIDE, chip).start()
        return c

    lax.fori_loop(1, chips, t_start, 0)
    x_copies[0].wait_recv()
    for d in range(chips):
        merged[d] = (f[:, d:d + 1] * partial[core, d].astype(F32)
                     + f[:, chips + d:chips + d + 1] * partial_in[d].astype(F32)).astype(BF16)

    def p_start(i, c):
        i = (5 * i) % chips
        p_copy(((x + i // SIDE) % SIDE) * SIDE + (y + i % SIDE) % SIDE, chip).start()
        return c

    lax.fori_loop(1, chips, p_start, 0)
    parts[chip] = merged[chip]
    tops_all[chip] = tops_out[chip]

    def t_wait(i, c):
        s = (chip + i) % chips
        t_copy(s, s).wait_recv()
        return c

    lax.fori_loop(1, chips, t_wait, 0)
    top = tops_all[:, 0, :]
    f = jnp.exp2(top - jnp.max(top, axis=0, keepdims=True))
    f = columns(f / jnp.sum(f, axis=0, keepdims=True))

    def p_wait(i, c):
        s = (chip + i) % chips
        p_copy(s, s).wait_recv()
        return c

    lax.fori_loop(1, chips, p_wait, 0)
    acc = jnp.zeros((128, width), F32)
    for s in range(chips):
        acc += f[:, s:s + 1] * parts[s].astype(F32)
    flat[...] = acc
    pair_rows = 2 * own
    here = pl.ds(chip * pair_rows, pair_rows)
    for h in range(half):
        attended[core, here, h * width:(h + 1) * width] = flat[pl.ds(h, pair_rows, stride=half), :].astype(BF16)

    def at_copy(d, s):
        at = pl.ds(s * pair_rows, pair_rows)
        return remote(attended.at[core, at], attended.at[core, at], ag2_send.at[d], ag2_recv.at[s], (row, 2 * d + core))

    def at_relay(s, c):
        at = pl.ds(s * pair_rows, pair_rows)
        return remote(attended.at[c, at], attended.at[c, at], fw2_send.at[s], fw2_recv.at[s], partner)

    spread(at_copy, None, at_relay)
    cols = half * width
    terms[...] = (lax.dot_general(attended[0], wo[:, :cols], NT, preferred_element_type=F32)
                  + lax.dot_general(attended[1], wo[:, cols:], NT, preferred_element_type=F32))
    out_rows = out_ref.shape[0]

    def z_copy(z, s):
        return remote(terms.at[pl.ds(z * out_rows, out_rows)], summed.at[s], z_send.at[z], z_recv.at[s], (z, me))

    for i in range(1, planes):
        z_copy((row + i) % planes, row).start()

    def pair_sent(d, c):
        pair_copy(d).wait_send()
        return c

    lax.fori_loop(0, chips, pair_sent, 0)
    for o in (1, 2, 3):
        a_copy((x + o) % SIDE, x).wait_send()
        for i in range(SIDE):
            b_copy((y + o) % SIDE, i, y).wait_send()
        a2_copy((y + o) % SIDE, y).wait_send()
        b2_copy((x + o) % SIDE, x).wait_send()

    def ent_sent(i, c):
        ent_copy((me + i) % peers, me).wait_send()
        return c

    lax.fori_loop(1, peers, ent_sent, 0)
    spread_end(q_copy, q_relay)
    for copy in x_copies:
        copy.wait_send()

    def tp_sent(i, c):
        d = (chip + i) % chips
        t_copy(d, chip).wait_send()
        p_copy(d, chip).wait_send()
        return c

    lax.fori_loop(1, chips, tp_sent, 0)
    spread_end(at_copy, at_relay)

    result = terms[pl.ds(row * out_rows, out_rows), :]
    for i in range(1, planes):
        z = (row + i) % planes
        z_copy(z, z).wait_recv()
        result += summed[z]
    out_ref[...] = result.astype(BF16)
    for i in range(1, planes):
        z_copy((row + i) % planes, row).wait_send()


def run(ht, w, dt, up, gain, freq, holder, index, used, tenant, held, k, v, wo, peers, planes):
    rows, wide, width = ht.shape[1], w.shape[1], gain.shape[1]
    own = rows // peers
    cap = 2 * own * holder.shape[1] // peers
    chips = peers // 2
    heads = wide // width
    blocks, toks, _ = k.shape
    slots = peers * cap
    count = -(-(slots // GROUP + blocks * (GROUP - 1) // GROUP) // UNROLL) * UNROLL
    positions = count * GROUP
    wide_a = (wide + 128) // 256 * 128 + 128
    wide_b = wide + 128 - wide_a
    cols = wo.shape[0]
    vm = pltpu.VMEM
    dma = pltpu.SemaphoreType.DMA
    args = (ht, w, dt, up, gain, freq, holder, index, used, tenant, held, k, v, wo)
    return pl.pallas_call(
        kernel,
        out_shape=jax.ShapeDtypeStruct((rows // planes, cols), BF16),
        in_specs=[pl.BlockSpec(memory_space=pltpu.HBM)] * len(args),
        out_specs=pl.BlockSpec(memory_space=pltpu.VMEM),
        scratch_shapes=[vm(a.shape, a.dtype) for a in args[:11]] + [
            pltpu.SMEM(tenant.shape, I32), pltpu.SMEM(held.shape, I32),
            vm(k.shape, BF16), vm(v.shape, BF16), vm(wo.shape, BF16),
            vm((rows, wide + 128), F32), vm((chips, own, wide + 128), F32),
            vm((SIDE, SIDE, own, wide_a), F32), vm((SIDE, SIDE, own, wide_b), F32),
            vm((SIDE, SIDE, own, wide_a), F32), vm((SIDE, SIDE, own, wide_b), F32),
            vm((SIDE, own, wide_a), F32), vm((SIDE, own, wide_b), F32),
            vm((SIDE, own, wide_a), F32), vm((SIDE, own, wide_b), F32),
            vm((own, wide + 128), F32), vm((128 // up.shape[1], up.shape[1], 128), F32), vm((own, heads, width), F32),
            vm((slots, 128), BF16), vm((slots, 128), BF16), vm((8, positions), I32), vm((8, slots), I32),
            pltpu.SMEM((8, positions), I32), pltpu.SMEM((8, slots), I32),
            vm((rows, heads, width), BF16),
            vm((positions, 2, heads // 2, width), F32), vm((positions, 2, heads // 2, width), F32),
            vm((2, chips, 128, width), BF16), vm((2, chips, 128), F32),
            vm((chips, 128, width), BF16), vm((chips, 128), F32),
            vm((chips, 128, width), BF16), vm((chips, 8, 128), F32),
            vm((chips, 128, width), BF16), vm((chips, 8, 128), F32), vm((128, width), F32),
            vm((2, rows, wide // 2), BF16), vm((rows, cols), F32), vm((planes, rows // planes, cols), F32),
            dma((14,)), dma((2 * PIECES,)), dma((2,)), dma((chips,)), dma((chips,)),
            dma((SIDE,)), dma((SIDE,)), dma((SIDE, SIDE)), dma((SIDE, SIDE)),
            dma((SIDE,)), dma((SIDE,)), dma((SIDE,)), dma((SIDE,)),
            dma((peers,)), dma((peers,)), dma((chips,)), dma((chips,)), dma((chips,)), dma((chips,)),
            dma((2,)), dma((2,)), dma((chips,)), dma((chips,)), dma((chips,)), dma((chips,)),
            dma((chips,)), dma((chips,)), dma((chips,)), dma((chips,)), dma((planes,)), dma((planes,)),
        ],
        compiler_params=pltpu.CompilerParams(
            vmem_limit_bytes=62 * 2**20, collective_id=0, has_side_effects=True),
        name="decode",
    )(*args)


def local(hidden, query_weight, adapter_down_weight, adapter_up_weight, query_norm_gain, paged_key_cache,
          paged_value_cache, output_weight, holder, holder_block_index, block_used_length, tenant, tenant_adapter):
    peers, planes = lax.axis_size("kv"), lax.axis_size("row")
    count, _, rank = adapter_down_weight.shape
    width = query_norm_gain.shape[0]
    blocks, toks, kv_heads, _ = paged_key_cache.shape
    half = width // 2
    freq = ROPE_BASE ** (-(jnp.arange(half, dtype=jnp.float32) * 2.0) / width)
    freq = jnp.concatenate([freq, freq])[None, :]
    down = jnp.transpose(adapter_down_weight, (0, 2, 1)).reshape(count * rank, -1)
    pool = (blocks, toks * kv_heads, width)
    return run(hidden.T, query_weight, down, adapter_up_weight, query_norm_gain[None, :], freq, holder,
               holder_block_index, block_used_length, tenant[None, :], tenant_adapter[None, :],
               paged_key_cache.reshape(pool), paged_value_cache.reshape(pool), output_weight.T, peers, planes)


def solution(mesh):
    return jax.shard_map(
        local,
        mesh=mesh,
        in_specs=(
            P(None, "kv"),
            P("kv", "row"),
            P(None, "kv", None),
            P(None, None, "row"),
            P(),
            P("kv", None, "row", None),
            P("kv", None, "row", None),
            P("row", "kv"),
            P("kv", None),
            P("kv", None),
            P("kv", None),
            P(),
            P(),
        ),
        out_specs=P("row", "kv"),
        check_vma=False,
    )
```

time: 572 us -> 88.4 us (0.15)
  matrix products: 176 us -> 0 us
  blocking collectives: 123 us -> 0 us
  waiting for transfers between devices: 120 us -> 0 us
  Pallas kernels: 0 us -> 86.2 us
  local copies, waits for them, and re-layouts: 74.1 us -> 1.38 us
  starting transfers between devices: 37.5 us -> 0 us
  other arithmetic: 20.6 us -> 0.6 us
  between operations: 14.4 us -> 0.01 us
    dot_general x12 -> x0, matrix products: 176 us -> none  [the longest x1 85.2 us: local(): jnp.einsum('rajd,rtad->rajt', grouped, keys, preferred_element_type=jnp.f...]
    unnamed x1 -> x0, blocking collectives: 123 us -> none
    pallas_call x0 -> x1, Pallas kernels: none -> 86.2 us  [run(): pl.pallas_call(kernel, out_shape=jax.ShapeDtypeStruct((rows // planes, co...]
    all_to_all x5 -> x0, waiting for transfers between devices: 57.7 us -> none  [the longest x1 46.4 us: local(): lax.all_to_all(block_out, 'kv', split_axis=0, concat_axis=0, tiled=True)]
    all_gather x1 -> x0, waiting for transfers between devices: 45.1 us -> none  [local(): lax.all_gather(attention, 'kv', axis=0, tiled=True)]
    reshape x11 -> x0, local copies, waits for them, and re-layouts: 40.7 us -> none  [the longest x1 14.4 us: local(): paged_key_cache.reshape(local_blocks, block_size * kv_local * head_size)]
    all_to_all x5 -> x0, starting transfers between devices: 37.2 us -> none  [the longest x1 9.32 us: local(): lax.all_to_all(sent_queries, 'kv', split_axis=0, concat_axis=0, tiled=True)]
    dot_general x3 -> x0, local copies, waits for them, and re-layouts: 24 us -> none  [the longest x1 11.9 us: local(): jnp.dot(block_pick, flat_values, preferred_element_type=jnp.bfloat16)]
  transfers between devices with their start and end apart: 8 -> 0, of which waited for: 4 -> 0; matrix products, arithmetic and copies ran while one was open for 24% -> 0% of each run, Pallas kernels for 0% -> 0%
where the time goes in v2:
time: 88.4 us; the launch traced here: 88.2 us
  Pallas kernels  86.2 us (98%)
  local copies, waits for them, and re-layouts  1.38 us (2%)
    pallas_call x1, Pallas kernels, run(): pl.pallas_call(kernel, out_shape=jax.ShapeDtypeStruct((rows // planes, co...  86.2 us

profile of v2, /device:TPU:1, one launch (start us, length us, event | category | flops | bytes accessed | tf_op | source)
XLA Modules:
  0.0 88.2 jit_solution(15481957058700866520)
XLA Ops:
  0.0 0.6 maximum_bitcast_fusion.freq_h
  0.6 86.2 %decode.1 = bf16[64,160]{1,0:T(8,128)(2,1)} custom-call(bf16[160,256]{1,0:T(8,128)(2,1)} %bitcast.16, bf16[160,2048]{1,0:T(8,128)(2,1)} %w_h.1, bf16[512,160]{1,0:T(8,128)(2,1)} %bitcast.15, f32[32,16,2048]{2,1,0:T(8,128)} %up_h.1, f32[1,128]{1,0:T(1,128)} %bitcast.18, f32[1,128]{1,0:T(1,128)} %maximum_bitcast_fusion.freq_h, s32[8,32]{1,0:T(8,128)} %holder_h.1, ...), custom_call_target="tpu_custom_call" | custom-call | tf_op jit(solution)/shard_map/decode/pallas_call | solution.py:510
  86.8 1.4 %copy.15 = bf16[64,160]{1,0:T(8,128)(2,1)} copy(bf16[64,160]{1,0:T(8,128)(2,1)} %decode.1) | data formatting | bytes 40960
  (1 shorter events, 0.0 us)

commit v3 on v2

--- a/solution.py
+++ b/solution.py
@@ -15,8 +15,8 @@
 TT = (((0,), (1,)), ((), ()))
 MESH = pl.DeviceIdType.MESH
 PIECES = 4
-GROUP = 8
-UNROLL = 16
+GROUP = 4
+UNROLL = 56
 SIDE = 4
 ADAPTER_SCALE = 0.5
 ROPE_BASE = 1000000.0
@@ -79,7 +79,7 @@
     chosen = jnp.where(place == iota((slots, positions), 1).astype(F32), 1.0, 0.0).astype(BF16)
     table = jnp.dot(fields, chosen, preferred_element_type=F32)[0:8]
     sub = iota(table.shape, 0)
-    table = jnp.where(sub == 1, 2.0 * table, table).astype(I32)
+    table = table.astype(I32)
     table = jnp.clip(table, 0, jnp.where(sub == 0, blocks - 1, jnp.where(sub == 1, 1 << 16, rows - 1)))
     lane = iota((slots, 128), 1)
     seats = jnp.where(lane == 0, chunk_c, jnp.where(lane == 1, seat_c, 0.0)).astype(BF16)
@@ -94,13 +94,13 @@
 
 def kernel(ht_h, w_h, dt_h, up_h, gain_h, freq_h, holder_h, index_h, used_h, tenant_h, held_h, k_h, v_h, wo_h,
            out_ref,
-           ht, w, dt, up, gain, freq, holder, index, used, tenant, held, tenant_s, held_s, kbuf, vbuf, wo,
+           ht, w, dt, up, gain, freq, holder, index, used, tenant, held, tenant_s, held_s, kbuf, vbuf, wo, wo_in,
            part, pair, mine_a, mine_b, land_a, land_b, sum_a, sum_b, end_a, end_b, total, low_t, turned,
            ent_send, ent, tab_v, slot_v, tab, slot_s, q, o_st, e_st,
            partial, tops, partial_in, tops_in, merged, tops_out, parts, tops_all, flat, attended, terms, summed,
            in_sem, kv_sem, tab_sem, pair_send, pair_recv, a_send, a_recv, b_send, b_recv, a2_send, a2_recv,
            b2_send, b2_recv, en_send, en_recv, ag_send, ag_recv, fw_send, fw_recv,
-           x_send, x_recv, p_send, p_recv, t_send, t_recv, ag2_send, ag2_recv, fw2_send, fw2_recv, z_send, z_recv):
+           wo_send, wo_recv, x_send, x_recv, p_send, p_recv, t_send, t_recv, ag2_send, ag2_recv, z_send, z_recv):
     row, me = lax.axis_index("row"), lax.axis_index("kv")
     peers, planes = lax.axis_size("kv"), lax.axis_size("row")
     chips = peers // 2
@@ -121,6 +121,7 @@
 
     def greet_plane(i, c):
         pl.semaphore_signal(barrier, inc=1, device_id=((row + i) % planes, me), device_id_type=MESH)
+        pl.semaphore_signal(barrier, inc=1, device_id=((row + i) % planes, partner[1]), device_id_type=MESH)
         return c
 
     lax.fori_loop(1, peers, greet, 0)
@@ -129,7 +130,7 @@
     loads = [pltpu.make_async_copy(src, dst, in_sem.at[i]) for i, (src, dst) in enumerate((
         (ht_h, ht), (w_h, w), (holder_h, holder), (index_h, index), (used_h, used), (tenant_h, tenant),
         (held_h, held), (dt_h, dt), (tenant_h, tenant_s), (held_h, held_s), (gain_h, gain), (freq_h, freq),
-        (up_h, up), (wo_h, wo)))]
+        (up_h, up), (wo_h.at[:, :wide // 2], wo.at[0]), (wo_h.at[:, wide // 2:], wo.at[1])))]
     for copy in loads:
         copy.start()
     step = blocks // PIECES
@@ -154,7 +155,7 @@
     part[:, wide:] = sum(low[:, 128 * i: 128 * (i + 1)] for i in range(low.shape[1] // 128))
     ent_send[...] = entries_by_holder(holder[...], index[...], used[...], me, own, peers, cap)
 
-    pl.semaphore_wait(barrier, peers + planes - 2)
+    pl.semaphore_wait(barrier, peers - 1 + 2 * (planes - 1))
 
     def pair_copy(d):
         return remote(part.at[pl.ds((2 * d + 1 - core) * own, own)], pair.at[d],
@@ -205,6 +206,18 @@
     angles = (jnp.sum(used[...], axis=1, keepdims=True) - 1).astype(F32) * freq[...]
     cosine, sine = jnp.cos(angles), jnp.sin(angles)
     sine = jnp.where(iota(sine.shape, 1) < width // 2, -sine, sine)
+
+    wo_copy = remote(wo.at[1 - core], wo_in, wo_send, wo_recv, partner)
+    wo_copy.start()
+
+    for copy in pool:
+        copy.wait()
+
+    def turn_keys(b, c):
+        kbuf[b] = jnp.transpose(kbuf[b].reshape(toks // 2, 2 * width))
+        return c
+
+    lax.fori_loop(0, blocks, turn_keys, 0, unroll=4)
 
     def a2_copy(t, s):
         return remote(sum_a.at[t], end_a.at[s], a2_send.at[t], a2_recv.at[s], (row, 2 * (x * SIDE + t) + core))
@@ -259,39 +272,11 @@
         turned[:, h, :] = t * cosine + pltpu.roll(t, width // 2, 1) * sine
     q[pl.ds(me * own, own)] = turned[...].astype(BF16)
 
-    def spread(copy_of, first_ref, relay_copy):
-        def start(i, c):
-            i = (5 * i) % chips
-            copy_of(((x + i // SIDE) % SIDE) * SIDE + (y + i % SIDE) % SIDE, chip).start()
-            return c
-
-        def relay(i, c):
-            i = (5 * i) % chips
-            s = ((x + SIDE - i // SIDE) % SIDE) * SIDE + (y + SIDE - i % SIDE) % SIDE
-            copy_of(s, s).wait_recv()
-            relay_copy(s, core).start()
-            return c
-
-        def landed(d, c):
-            relay_copy(d, 1 - core).wait_recv()
-            return c
-
-        lax.fori_loop(1, chips, start, 0)
-        relay_copy(chip, core).start()
-        lax.fori_loop(1, chips, relay, 0)
-        lax.fori_loop(0, chips, landed, 0)
-
-    def spread_end(copy_of, relay_copy):
-        def sent(i, c):
-            copy_of((chip + i) % chips, chip).wait_send()
-            return c
-
-        def relayed(d, c):
-            relay_copy(d, core).wait_send()
-            return c
-
-        lax.fori_loop(1, chips, sent, 0)
-        lax.fori_loop(0, chips, relayed, 0)
+    def chip_by(i, sign):
+        dx, dy = i // SIDE, i % SIDE
+        return ((x + sign * dx + SIDE) % SIDE) * SIDE + (y + sign * dy + SIDE) % SIDE
+
+    far = sorted(range(1, chips), key=lambda i: -(min(i // SIDE, SIDE - i // SIDE) + min(i % SIDE, SIDE - i % SIDE)))
 
     def q_copy(d, s):
         at = pl.ds((2 * s + core) * own, own)
@@ -301,29 +286,66 @@
         at = pl.ds((2 * s + c) * own, own)
         return remote(q.at[at], q.at[at], fw_send.at[s], fw_recv.at[s], partner)
 
-    spread(q_copy, None, q_relay)
+    for i in far:
+        q_copy(chip_by(i, 1), chip).start()
+    q_relay(chip, core).start()
+
+    def turn_values(b, c):
+        both = vbuf[b].reshape(toks // 2, 2 * width)
+        vbuf[b, :toks // 2] = both[:, :width]
+        vbuf[b, toks // 2:] = both[:, width:]
+        return c
+
+    lax.fori_loop(0, blocks, turn_values, 0, unroll=4)
+
+    def pair_sent(d, c):
+        pair_copy(d).wait_send()
+        return c
+
+    lax.fori_loop(0, chips, pair_sent, 0)
+    for o in (1, 2, 3):
+        a_copy((x + o) % SIDE, x).wait_send()
+        for i in range(SIDE):
+            b_copy((y + o) % SIDE, i, y).wait_send()
+        a2_copy((y + o) % SIDE, y).wait_send()
+        b2_copy((x + o) % SIDE, x).wait_send()
     for copy in tables:
         copy.wait()
-    for copy in pool:
-        copy.wait()
+
+    for i in far:
+        s = chip_by(i, -1)
+        q_copy(s, s).wait_recv()
+        q_relay(s, core).start()
+
+    def q_landed(d, c):
+        q_relay(d, 1 - core).wait_recv()
+        return c
+
+    lax.fori_loop(0, chips, q_landed, 0)
 
     coef = math.log2(math.e) / math.sqrt(width)
-    col = iota((heads, toks), 1)
-    col = jnp.where((col & 1) == lax.div(iota((heads, toks), 0), heads // 2), col, 1 << 20)
+    half = heads // 2
+    col = iota((heads, toks // 2), 1)
+    upper = iota((heads, width), 0) < half
+    none = jnp.zeros((heads, width), BF16)
 
     def chunk(c):
         base = c * GROUP
         b = tab[0, base]
-        qs = jnp.concatenate([q[tab[2, base + g]] for g in range(GROUP)], axis=0)
-        s = lax.dot_general(qs, kbuf[b], NT, preferred_element_type=F32)
+        qs = [q[tab[2, base + g]] for g in range(GROUP)]
+        qs = jnp.concatenate([jnp.concatenate(
+            [jnp.where(upper, one, none), jnp.where(upper, none, one)], axis=1) for one in qs], axis=0)
+        s = jnp.dot(qs, kbuf[b], preferred_element_type=F32)
         s = jnp.concatenate(
             [jnp.where(col < tab[1, base + g], s[heads * g: heads * (g + 1)], NEG) for g in range(GROUP)], axis=0)
         m = jnp.max(s, axis=1, keepdims=True)
         wt = jnp.exp2((s - m) * coef)
         l = jnp.sum(wt, axis=1, keepdims=True)
-        o = jnp.dot(wt.astype(BF16), vbuf[b], preferred_element_type=F32) / l
+        vs = jnp.concatenate([vbuf[b, :toks // 2], vbuf[b, toks // 2:]], axis=1)
+        o = jnp.dot(wt.astype(BF16), vs, preferred_element_type=F32).reshape(GROUP, 2, half, 2 * width)
+        o = jnp.concatenate([o[:, 0:1, :, :width], o[:, 1:2, :, width:]], axis=1).reshape(GROUP * heads, width) / l
         e = jnp.broadcast_to(m * coef + jnp.log2(l), o.shape)
-        return o.reshape(GROUP, 2, heads // 2, width), e.reshape(GROUP, 2, heads // 2, width)
+        return o.reshape(GROUP, 2, half, width), e.reshape(GROUP, 2, half, width)
 
     def chunks(i, c):
         done = [chunk(i * UNROLL + u) for u in range(UNROLL)]
@@ -336,92 +358,121 @@
 
     lax.fori_loop(0, tab.shape[1] // (GROUP * UNROLL), chunks, 0)
 
-    half = heads // 2
     lane = iota((half, 128), 1)
     same_head = (lane & (half - 1)) == iota((half, 128), 0)
     lane_row = jnp.where(same_head, lax.div(lane, half), -2)
     slots = 2 * cap
 
-    def merge(d, c):
-        for hv in range(2):
-            tops_of, outs = [], []
-            for p in range(slots):
-                at = slot_s[0, d * slots + p]
-                tops_of.append(jnp.where(lane_row == slot_s[1, d * slots + p], e_st[at, hv], NEG))
-                outs.append(o_st[at, hv])
-            es = jnp.concatenate(tops_of, axis=0)
-            top = jnp.max(es, axis=0, keepdims=True)
-            f = jnp.exp2(es - top)
-            l = jnp.sum(f, axis=0, keepdims=True)
-            f = (f * (1.0 / l)).astype(BF16)
-            os = jnp.concatenate(outs, axis=0).astype(BF16)
-            partial[hv, d] = lax.dot_general(f, os, TN, preferred_element_type=F32).astype(BF16)
-            tops[hv, pl.ds(d, 1), :] = top + jnp.log2(l)
-        return c
-
-    lax.fori_loop(0, chips, merge, 0)
-
-    x_copies = (remote(partial.at[1 - core], partial_in, x_send.at[0], x_recv.at[0], partner),
-                remote(tops.at[1 - core], tops_in, x_send.at[1], x_recv.at[1], partner))
-    for copy in x_copies[::-1]:
-        copy.start()
+    def merge(d, hv):
+        tops_of, outs = [], []
+        for p in range(slots):
+            at = slot_s[0, d * slots + p]
+            tops_of.append(jnp.where(lane_row == slot_s[1, d * slots + p], e_st[at, hv], NEG))
+            outs.append(o_st[at, hv])
+        es = jnp.concatenate(tops_of, axis=0)
+        top = jnp.max(es, axis=0, keepdims=True)
+        f = jnp.exp2(es - top)
+        l = jnp.sum(f, axis=0, keepdims=True)
+        f = (f * (1.0 / l)).astype(BF16)
+        os = jnp.concatenate(outs, axis=0).astype(BF16)
+        return lax.dot_general(f, os, TN, preferred_element_type=F32).astype(BF16), top + jnp.log2(l)
+
+    many = chips // PIECES
+
+    def x_copy(i):
+        at = pl.ds(i * many, many)
+        return remote(partial.at[1 - core, at], partial_in.at[at], x_send.at[i], x_recv.at[i], partner)
+
+    tops_copy = remote(tops.at[1 - core], tops_in, x_send.at[PIECES], x_recv.at[PIECES], partner)
+
+    for hv in (1 - core, core):
+        def merges(i, c, hv=hv):
+            done = [merge(i * many + u, hv) for u in range(many)]
+            for u in range(many):
+                partial[hv, i * many + u] = done[u][0]
+                tops[hv, pl.ds(i * many + u, 1), :] = done[u][1]
+            return c
+
+        def merges_sent(i, c):
+            merges(i, c)
+            x_copy(i).start()
+            return c
+
+        if hv is not core:
+            lax.fori_loop(0, PIECES, merges_sent, 0)
+            tops_copy.start()
+        else:
+            lax.fori_loop(0, PIECES, merges, 0)
 
     def columns(fs):
         n = fs.shape[0]
         return jnp.transpose(jnp.concatenate([fs, jnp.zeros((128 - n, 128), F32)], axis=0))
 
-    x_copies[1].wait_recv()
-    t0, t1 = tops[core], tops_in[...]
+    order = far + [0]
+    tops_copy.wait_recv()
+    t0 = jnp.concatenate([tops[core, pl.ds(chip_by(i, 1), 1), :] for i in order], axis=0)
+    t1 = jnp.concatenate([tops_in[pl.ds(chip_by(i, 1), 1), :] for i in order], axis=0)
     top = jnp.maximum(t0, t1)
     f0, f1 = jnp.exp2(t0 - top), jnp.exp2(t1 - top)
     l = f0 + f1
     over = top + jnp.log2(l)
-    for d in range(chips):
-        tops_out[d] = jnp.broadcast_to(over[d:d + 1], (8, 128))
+    for k in range(chips):
+        tops_out[k] = jnp.broadcast_to(over[k:k + 1], (8, 128))
     f = columns(jnp.concatenate([f0 / l, f1 / l], axis=0))
 
-    def t_copy(d, s):
-        return remote(tops_out.at[d], tops_all.at[s], t_send.at[d], t_recv.at[s], (row, 2 * d + core))
-
-    def p_copy(d, s):
-        return remote(merged.at[d], parts.at[s], p_send.at[d], p_recv.at[s], (row, 2 * d + core))
-
-    def t_start(i, c):
-        i = (5 * i) % chips
-        t_copy(((x + i // SIDE) % SIDE) * SIDE + (y + i % SIDE) % SIDE, chip).start()
-        return c
-
-    lax.fori_loop(1, chips, t_start, 0)
-    x_copies[0].wait_recv()
-    for d in range(chips):
-        merged[d] = (f[:, d:d + 1] * partial[core, d].astype(F32)
-                     + f[:, chips + d:chips + d + 1] * partial_in[d].astype(F32)).astype(BF16)
-
-    def p_start(i, c):
-        i = (5 * i) % chips
-        p_copy(((x + i // SIDE) % SIDE) * SIDE + (y + i % SIDE) % SIDE, chip).start()
-        return c
-
-    lax.fori_loop(1, chips, p_start, 0)
-    parts[chip] = merged[chip]
-    tops_all[chip] = tops_out[chip]
-
-    def t_wait(i, c):
-        s = (chip + i) % chips
-        t_copy(s, s).wait_recv()
-        return c
-
-    lax.fori_loop(1, chips, t_wait, 0)
+    def t_copy(k, d, s):
+        return remote(tops_out.at[k], tops_all.at[s], t_send.at[k], t_recv.at[s], (row, 2 * d + core))
+
+    def p_copy(k, d, s):
+        return remote(merged.at[k], parts.at[s], p_send.at[k], p_recv.at[s], (row, 2 * d + core))
+
+    for k, i in enumerate(order):
+        if i:
+            t_copy(k, chip_by(i, 1), chip).start()
+    for i in range(PIECES):
+        x_copy(i).wait_recv()
+    for k, i in enumerate(order):
+        d = chip_by(i, 1)
+        both = (f[:, k:k + 1] * partial[core, d].astype(F32)
+                + f[:, chips + k:chips + k + 1] * partial_in[d].astype(F32)).astype(BF16)
+        if i:
+            merged[k] = both
+            p_copy(k, d, chip).start()
+        else:
+            parts[chip] = both
+            tops_all[chip] = tops_out[k]
+
+    def ent_sent(i, c):
+        ent_copy((me + i) % peers, me).wait_send()
+        return c
+
+    lax.fori_loop(1, peers, ent_sent, 0)
+
+    def q_sent(i, c):
+        q_copy((chip + i) % chips, chip).wait_send()
+        return c
+
+    lax.fori_loop(1, chips, q_sent, 0)
+
+    def q_relayed(d, c):
+        q_relay(d, core).wait_send()
+        return c
+
+    lax.fori_loop(0, chips, q_relayed, 0)
+    for i in range(PIECES):
+        x_copy(i).wait_send()
+    tops_copy.wait_send()
+    wo_copy.wait()
+
+    for i in far[::-1]:
+        s = chip_by(i, -1)
+        t_copy(0, s, s).wait_recv()
     top = tops_all[:, 0, :]
     f = jnp.exp2(top - jnp.max(top, axis=0, keepdims=True))
     f = columns(f / jnp.sum(f, axis=0, keepdims=True))
-
-    def p_wait(i, c):
-        s = (chip + i) % chips
-        p_copy(s, s).wait_recv()
-        return c
-
-    lax.fori_loop(1, chips, p_wait, 0)
+    for i in far[::-1]:
+        s = chip_by(i, -1)
+        p_copy(0, s, s).wait_recv()
     acc = jnp.zeros((128, width), F32)
     for s in range(chips):
         acc += f[:, s:s + 1] * parts[s].astype(F32)
@@ -429,66 +480,45 @@
     pair_rows = 2 * own
     here = pl.ds(chip * pair_rows, pair_rows)
     for h in range(half):
-        attended[core, here, h * width:(h + 1) * width] = flat[pl.ds(h, pair_rows, stride=half), :].astype(BF16)
+        attended[here, h * width:(h + 1) * width] = flat[pl.ds(h, pair_rows, stride=half), :].astype(BF16)
 
     def at_copy(d, s):
         at = pl.ds(s * pair_rows, pair_rows)
-        return remote(attended.at[core, at], attended.at[core, at], ag2_send.at[d], ag2_recv.at[s], (row, 2 * d + core))
-
-    def at_relay(s, c):
-        at = pl.ds(s * pair_rows, pair_rows)
-        return remote(attended.at[c, at], attended.at[c, at], fw2_send.at[s], fw2_recv.at[s], partner)
-
-    spread(at_copy, None, at_relay)
-    cols = half * width
-    terms[...] = (lax.dot_general(attended[0], wo[:, :cols], NT, preferred_element_type=F32)
-                  + lax.dot_general(attended[1], wo[:, cols:], NT, preferred_element_type=F32))
+        return remote(attended.at[at], attended.at[at], ag2_send.at[d], ag2_recv.at[s], (row, 2 * d + core))
+
+    for i in far:
+        at_copy(chip_by(i, 1), chip).start()
+    for k, i in enumerate(far):
+        t_copy(k, chip_by(i, 1), chip).wait_send()
+        p_copy(k, chip_by(i, 1), chip).wait_send()
+    for i in far[::-1]:
+        s = chip_by(i, -1)
+        at_copy(s, s).wait_recv()
     out_rows = out_ref.shape[0]
 
-    def z_copy(z, s):
-        return remote(terms.at[pl.ds(z * out_rows, out_rows)], summed.at[s], z_send.at[z], z_recv.at[s], (z, me))
-
-    for i in range(1, planes):
-        z_copy((row + i) % planes, row).start()
-
-    def pair_sent(d, c):
-        pair_copy(d).wait_send()
-        return c
-
-    lax.fori_loop(0, chips, pair_sent, 0)
-    for o in (1, 2, 3):
-        a_copy((x + o) % SIDE, x).wait_send()
-        for i in range(SIDE):
-            b_copy((y + o) % SIDE, i, y).wait_send()
-        a2_copy((y + o) % SIDE, y).wait_send()
-        b2_copy((x + o) % SIDE, x).wait_send()
-
-    def ent_sent(i, c):
-        ent_copy((me + i) % peers, me).wait_send()
-        return c
-
-    lax.fori_loop(1, peers, ent_sent, 0)
-    spread_end(q_copy, q_relay)
-    for copy in x_copies:
-        copy.wait_send()
-
-    def tp_sent(i, c):
-        d = (chip + i) % chips
-        t_copy(d, chip).wait_send()
-        p_copy(d, chip).wait_send()
-        return c
-
-    lax.fori_loop(1, chips, tp_sent, 0)
-    spread_end(at_copy, at_relay)
-
-    result = terms[pl.ds(row * out_rows, out_rows), :]
-    for i in range(1, planes):
-        z = (row + i) % planes
-        z_copy(z, z).wait_recv()
-        result += summed[z]
+    def z_copy(c, z, s):
+        return remote(terms.at[c, pl.ds(z * out_rows, out_rows)], summed.at[c, s], z_send.at[c, z], z_recv.at[c, s],
+                      (z, partner[1] if c else me))
+
+    terms[1] = lax.dot_general(attended[...], wo_in[...], NT, preferred_element_type=F32)
+    for i in (2, 1, 3, 0):
+        z_copy(1, (row + i) % planes, row).start()
+    terms[0] = lax.dot_general(attended[...], wo[core], NT, preferred_element_type=F32)
+    for i in (2, 1, 3):
+        z_copy(0, (row + i) % planes, row).start()
+    for i in far:
+        at_copy(chip_by(i, 1), chip).wait_send()
+
+    result = terms[0, pl.ds(row * out_rows, out_rows), :]
+    for c in (1, 0):
+        for i in range(c ^ 1, planes):
+            z = (row + i) % planes
+            z_copy(c, z, z).wait_recv()
+            result += summed[c, z]
     out_ref[...] = result.astype(BF16)
-    for i in range(1, planes):
-        z_copy((row + i) % planes, row).wait_send()
+    for c in (1, 0):
+        for i in range(c ^ 1, planes):
+            z_copy(c, (row + i) % planes, row).wait_send()
 
 
 def run(ht, w, dt, up, gain, freq, holder, index, used, tenant, held, k, v, wo, peers, planes):
@@ -514,7 +544,7 @@
         out_specs=pl.BlockSpec(memory_space=pltpu.VMEM),
         scratch_shapes=[vm(a.shape, a.dtype) for a in args[:11]] + [
             pltpu.SMEM(tenant.shape, I32), pltpu.SMEM(held.shape, I32),
-            vm(k.shape, BF16), vm(v.shape, BF16), vm(wo.shape, BF16),
+            vm(k.shape, BF16), vm(v.shape, BF16), vm((2, cols, wide // 2), BF16), vm((cols, wide // 2), BF16),
             vm((rows, wide + 128), F32), vm((chips, own, wide + 128), F32),
             vm((SIDE, SIDE, own, wide_a), F32), vm((SIDE, SIDE, own, wide_b), F32),
             vm((SIDE, SIDE, own, wide_a), F32), vm((SIDE, SIDE, own, wide_b), F32),
@@ -529,13 +559,13 @@
             vm((chips, 128, width), BF16), vm((chips, 128), F32),
             vm((chips, 128, width), BF16), vm((chips, 8, 128), F32),
             vm((chips, 128, width), BF16), vm((chips, 8, 128), F32), vm((128, width), F32),
-            vm((2, rows, wide // 2), BF16), vm((rows, cols), F32), vm((planes, rows // planes, cols), F32),
-            dma((14,)), dma((2 * PIECES,)), dma((2,)), dma((chips,)), dma((chips,)),
+            vm((rows, wide // 2), BF16), vm((2, rows, cols), F32), vm((2, planes, rows // planes, cols), F32),
+            dma((15,)), dma((2 * PIECES,)), dma((2,)), dma((chips,)), dma((chips,)),
             dma((SIDE,)), dma((SIDE,)), dma((SIDE, SIDE)), dma((SIDE, SIDE)),
             dma((SIDE,)), dma((SIDE,)), dma((SIDE,)), dma((SIDE,)),
             dma((peers,)), dma((peers,)), dma((chips,)), dma((chips,)), dma((chips,)), dma((chips,)),
-            dma((2,)), dma((2,)), dma((chips,)), dma((chips,)), dma((chips,)), dma((chips,)),
-            dma((chips,)), dma((chips,)), dma((chips,)), dma((chips,)), dma((planes,)), dma((planes,)),
+            dma, dma, dma((PIECES + 1,)), dma((PIECES + 1,)), dma((chips,)), dma((chips,)), dma((chips,)), dma((chips,)),
+            dma((chips,)), dma((chips,)), dma((2, planes)), dma((2, planes)),
         ],
         compiler_params=pltpu.CompilerParams(
             vmem_limit_bytes=62 * 2**20, collective_id=0, has_side_effects=True),

time: 88.4 us -> 78.4 us (0.89)
  Pallas kernels: 86.2 us -> 76.2 us
    pallas_call x1, Pallas kernels: 86.2 us -> 76.2 us  [run(): pl.pallas_call(kernel, out_shape=jax.ShapeDtypeStruct((rows // planes, co...]
where the time goes in v3:
time: 78.4 us; the launch traced here: 78.2 us
  Pallas kernels  76.2 us (97%)
  local copies, waits for them, and re-layouts  1.38 us (2%)
    pallas_call x1, Pallas kernels, run(): pl.pallas_call(kernel, out_shape=jax.ShapeDtypeStruct((rows // planes, co...  76.2 us

profile of v3, /device:TPU:1, one launch (start us, length us, event | category | flops | bytes accessed | tf_op | source)
XLA Modules:
  0.0 78.2 jit_solution(513414541427907516)
XLA Ops:
  0.0 0.6 maximum_bitcast_fusion.freq_h
  0.6 76.2 %decode.1 = bf16[64,160]{1,0:T(8,128)(2,1)} custom-call(bf16[160,256]{1,0:T(8,128)(2,1)} %bitcast.16, bf16[160,2048]{1,0:T(8,128)(2,1)} %w_h.1, bf16[512,160]{1,0:T(8,128)(2,1)} %bitcast.15, f32[32,16,2048]{2,1,0:T(8,128)} %up_h.1, f32[1,128]{1,0:T(1,128)} %bitcast.18, f32[1,128]{1,0:T(1,128)} %maximum_bitcast_fusion.freq_h, s32[8,32]{1,0:T(8,128)} %holder_h.1, ...), custom_call_target="tpu_custom_call" | custom-call | tf_op jit(solution)/shard_map/decode/pallas_call | solution.py:540
  76.8 1.4 %copy.15 = bf16[64,160]{1,0:T(8,128)(2,1)} copy(bf16[64,160]{1,0:T(8,128)(2,1)} %decode.1) | data formatting | bytes 40960
  (1 shorter events, 0.0 us)

commit v4 on v3

--- a/solution.py
+++ b/solution.py
@@ -16,7 +16,7 @@
 MESH = pl.DeviceIdType.MESH
 PIECES = 4
 GROUP = 4
-UNROLL = 56
+UNROLL = 224
 SIDE = 4
 ADAPTER_SCALE = 0.5
 ROPE_BASE = 1000000.0
@@ -153,7 +153,6 @@
     adapter = jnp.transpose(adapter)[:, 0:1].astype(I32)
     low = jnp.where(lax.div(iota(low.shape, 1), rank) == adapter, low, 0.0)
     part[:, wide:] = sum(low[:, 128 * i: 128 * (i + 1)] for i in range(low.shape[1] // 128))
-    ent_send[...] = entries_by_holder(holder[...], index[...], used[...], me, own, peers, cap)
 
     pl.semaphore_wait(barrier, peers - 1 + 2 * (planes - 1))
 
@@ -169,6 +168,8 @@
         for oy in hops:
             dx, dy = chip_at(ox, oy)
             pair_copy(dx * SIDE + dy).start()
+
+    ent_send[...] = entries_by_holder(holder[...], index[...], used[...], me, own, peers, cap)
 
     def a_copy(t, s):
         return remote(mine_a.at[t], land_a.at[s], a_send.at[t], a_recv.at[s], (row, 2 * (t * SIDE + y) + core))
@@ -209,15 +210,6 @@
 
     wo_copy = remote(wo.at[1 - core], wo_in, wo_send, wo_recv, partner)
     wo_copy.start()
-
-    for copy in pool:
-        copy.wait()
-
-    def turn_keys(b, c):
-        kbuf[b] = jnp.transpose(kbuf[b].reshape(toks // 2, 2 * width))
-        return c
-
-    lax.fori_loop(0, blocks, turn_keys, 0, unroll=4)
 
     def a2_copy(t, s):
         return remote(sum_a.at[t], end_a.at[s], a2_send.at[t], a2_recv.at[s], (row, 2 * (x * SIDE + t) + core))
@@ -290,13 +282,17 @@
         q_copy(chip_by(i, 1), chip).start()
     q_relay(chip, core).start()
 
-    def turn_values(b, c):
+    def regroup(b, c):
+        kbuf[b] = jnp.transpose(kbuf[b].reshape(toks // 2, 2 * width))
         both = vbuf[b].reshape(toks // 2, 2 * width)
         vbuf[b, :toks // 2] = both[:, :width]
         vbuf[b, toks // 2:] = both[:, width:]
         return c
 
-    lax.fori_loop(0, blocks, turn_values, 0, unroll=4)
+    share = blocks // chips
+    for copy in pool:
+        copy.wait()
+    lax.fori_loop(0, share, regroup, 0, unroll=4)
 
     def pair_sent(d, c):
         pair_copy(d).wait_send()
@@ -312,10 +308,12 @@
     for copy in tables:
         copy.wait()
 
-    for i in far:
+    for i in far[::-1]:
         s = chip_by(i, -1)
         q_copy(s, s).wait_recv()
         q_relay(s, core).start()
+        at = (1 + far.index(i)) * share
+        lax.fori_loop(at, at + share, regroup, 0, unroll=4)
 
     def q_landed(d, c):
         q_relay(d, 1 - core).wait_recv()
@@ -377,39 +375,26 @@
         os = jnp.concatenate(outs, axis=0).astype(BF16)
         return lax.dot_general(f, os, TN, preferred_element_type=F32).astype(BF16), top + jnp.log2(l)
 
-    many = chips // PIECES
-
-    def x_copy(i):
-        at = pl.ds(i * many, many)
-        return remote(partial.at[1 - core, at], partial_in.at[at], x_send.at[i], x_recv.at[i], partner)
-
-    tops_copy = remote(tops.at[1 - core], tops_in, x_send.at[PIECES], x_recv.at[PIECES], partner)
-
-    for hv in (1 - core, core):
-        def merges(i, c, hv=hv):
-            done = [merge(i * many + u, hv) for u in range(many)]
-            for u in range(many):
-                partial[hv, i * many + u] = done[u][0]
-                tops[hv, pl.ds(i * many + u, 1), :] = done[u][1]
-            return c
-
-        def merges_sent(i, c):
-            merges(i, c)
-            x_copy(i).start()
-            return c
-
-        if hv is not core:
-            lax.fori_loop(0, PIECES, merges_sent, 0)
-            tops_copy.start()
-        else:
-            lax.fori_loop(0, PIECES, merges, 0)
+    def merges(hv):
+        done = [merge(d, hv) for d in range(chips)]
+        for d in range(chips):
+            partial[hv, d] = done[d][0]
+        tops[hv] = jnp.concatenate([one[1] for one in done], axis=0)
+
+    x_copies = (remote(tops.at[1 - core], tops_in, x_send.at[0], x_recv.at[0], partner),
+                remote(partial.at[1 - core], partial_in, x_send.at[1], x_recv.at[1], partner))
+
+    merges(1 - core)
+    for copy in x_copies:
+        copy.start()
+    merges(core)
 
     def columns(fs):
         n = fs.shape[0]
         return jnp.transpose(jnp.concatenate([fs, jnp.zeros((128 - n, 128), F32)], axis=0))
 
     order = far + [0]
-    tops_copy.wait_recv()
+    x_copies[0].wait_recv()
     t0 = jnp.concatenate([tops[core, pl.ds(chip_by(i, 1), 1), :] for i in order], axis=0)
     t1 = jnp.concatenate([tops_in[pl.ds(chip_by(i, 1), 1), :] for i in order], axis=0)
     top = jnp.maximum(t0, t1)
@@ -429,8 +414,7 @@
     for k, i in enumerate(order):
         if i:
             t_copy(k, chip_by(i, 1), chip).start()
-    for i in range(PIECES):
-        x_copy(i).wait_recv()
+    x_copies[1].wait_recv()
     for k, i in enumerate(order):
         d = chip_by(i, 1)
         both = (f[:, k:k + 1] * partial[core, d].astype(F32)
@@ -459,9 +443,8 @@
         return c
 
     lax.fori_loop(0, chips, q_relayed, 0)
-    for i in range(PIECES):
-        x_copy(i).wait_send()
-    tops_copy.wait_send()
+    for copy in x_copies:
+        copy.wait_send()
     wo_copy.wait()
 
     for i in far[::-1]:
@@ -500,21 +483,21 @@
         return remote(terms.at[c, pl.ds(z * out_rows, out_rows)], summed.at[c, s], z_send.at[c, z], z_recv.at[c, s],
                       (z, partner[1] if c else me))
 
-    terms[1] = lax.dot_general(attended[...], wo_in[...], NT, preferred_element_type=F32)
+    terms[1] = lax.dot_general(attended[...], wo_in[...], NT, preferred_element_type=F32).astype(BF16)
     for i in (2, 1, 3, 0):
         z_copy(1, (row + i) % planes, row).start()
-    terms[0] = lax.dot_general(attended[...], wo[core], NT, preferred_element_type=F32)
+    terms[0] = lax.dot_general(attended[...], wo[core], NT, preferred_element_type=F32).astype(BF16)
     for i in (2, 1, 3):
         z_copy(0, (row + i) % planes, row).start()
     for i in far:
         at_copy(chip_by(i, 1), chip).wait_send()
 
-    result = terms[0, pl.ds(row * out_rows, out_rows), :]
+    result = terms[0, pl.ds(row * out_rows, out_rows), :].astype(F32)
     for c in (1, 0):
         for i in range(c ^ 1, planes):
             z = (row + i) % planes
             z_copy(c, z, z).wait_recv()
-            result += summed[c, z]
+            result += summed[c, z].astype(F32)
     out_ref[...] = result.astype(BF16)
     for c in (1, 0):
         for i in range(c ^ 1, planes):
@@ -559,12 +542,12 @@
             vm((chips, 128, width), BF16), vm((chips, 128), F32),
             vm((chips, 128, width), BF16), vm((chips, 8, 128), F32),
             vm((chips, 128, width), BF16), vm((chips, 8, 128), F32), vm((128, width), F32),
-            vm((rows, wide // 2), BF16), vm((2, rows, cols), F32), vm((2, planes, rows // planes, cols), F32),
+            vm((rows, wide // 2), BF16), vm((2, rows, cols), BF16), vm((2, planes, rows // planes, cols), BF16),
             dma((15,)), dma((2 * PIECES,)), dma((2,)), dma((chips,)), dma((chips,)),
             dma((SIDE,)), dma((SIDE,)), dma((SIDE, SIDE)), dma((SIDE, SIDE)),
             dma((SIDE,)), dma((SIDE,)), dma((SIDE,)), dma((SIDE,)),
             dma((peers,)), dma((peers,)), dma((chips,)), dma((chips,)), dma((chips,)), dma((chips,)),
-            dma, dma, dma((PIECES + 1,)), dma((PIECES + 1,)), dma((chips,)), dma((chips,)), dma((chips,)), dma((chips,)),
+            dma, dma, dma((2,)), dma((2,)), dma((chips,)), dma((chips,)), dma((chips,)), dma((chips,)),
             dma((chips,)), dma((chips,)), dma((2, planes)), dma((2, planes)),
         ],
         compiler_params=pltpu.CompilerParams(

time: 78.4 us -> 74.5 us (0.950)
  Pallas kernels: 76.2 us -> 72.3 us
    pallas_call x1, Pallas kernels: 76.2 us -> 72.3 us  [run(): pl.pallas_call(kernel, out_shape=jax.ShapeDtypeStruct((rows // planes, co...]
where the time goes in v4:
time: 74.5 us; the launch traced here: 74.3 us
  Pallas kernels  72.3 us (97%)
  local copies, waits for them, and re-layouts  1.38 us (2%)
    pallas_call x1, Pallas kernels, run(): pl.pallas_call(kernel, out_shape=jax.ShapeDtypeStruct((rows // planes, co...  72.3 us

profile of v4, /device:TPU:1, one launch (start us, length us, event | category | flops | bytes accessed | tf_op | source)
XLA Modules:
  0.0 74.3 jit_solution(9544918557755471963)
XLA Ops:
  0.0 0.6 maximum_bitcast_fusion.freq_h
  0.6 72.3 %decode.1 = bf16[64,160]{1,0:T(8,128)(2,1)} custom-call(bf16[160,256]{1,0:T(8,128)(2,1)} %bitcast.16, bf16[160,2048]{1,0:T(8,128)(2,1)} %w_h.1, bf16[512,160]{1,0:T(8,128)(2,1)} %bitcast.15, f32[32,16,2048]{2,1,0:T(8,128)} %up_h.1, f32[1,128]{1,0:T(1,128)} %bitcast.18, f32[1,128]{1,0:T(1,128)} %maximum_bitcast_fusion.freq_h, s32[8,32]{1,0:T(8,128)} %holder_h.1, ...), custom_call_target="tpu_custom_call" | custom-call | tf_op jit(solution)/shard_map/decode/pallas_call | solution.py:523
  73.0 1.4 %copy.15 = bf16[64,160]{1,0:T(8,128)(2,1)} copy(bf16[64,160]{1,0:T(8,128)(2,1)} %decode.1) | data formatting | bytes 40960
  (1 shorter events, 0.0 us)

commit v5 on v4

--- a/solution.py
+++ b/solution.py
@@ -124,25 +124,24 @@
         pl.semaphore_signal(barrier, inc=1, device_id=((row + i) % planes, partner[1]), device_id_type=MESH)
         return c
 
-    lax.fori_loop(1, peers, greet, 0)
-    lax.fori_loop(1, planes, greet_plane, 0)
-
     loads = [pltpu.make_async_copy(src, dst, in_sem.at[i]) for i, (src, dst) in enumerate((
         (ht_h, ht), (w_h, w), (holder_h, holder), (index_h, index), (used_h, used), (tenant_h, tenant),
         (held_h, held), (dt_h, dt), (tenant_h, tenant_s), (held_h, held_s), (gain_h, gain), (freq_h, freq),
         (up_h, up), (wo_h.at[:, :wide // 2], wo.at[0]), (wo_h.at[:, wide // 2:], wo.at[1])))]
-    for copy in loads:
+    for copy in loads[:8]:
         copy.start()
+    lax.fori_loop(1, peers, greet, 0)
+    lax.fori_loop(1, planes, greet_plane, 0)
     step = blocks // PIECES
     pool = []
     for i in range(PIECES):
         at = pl.ds(i * step, step)
         pool += [pltpu.make_async_copy(k_h.at[at], kbuf.at[at], kv_sem.at[2 * i]),
                  pltpu.make_async_copy(v_h.at[at], vbuf.at[at], kv_sem.at[2 * i + 1])]
-    for copy in pool:
-        copy.start()
     for copy in loads[:8]:
         copy.wait()
+    for copy in loads[8:] + pool:
+        copy.start()
 
     part[:, :wide] = lax.dot_general(ht[...], w[...], TN, preferred_element_type=F32)
     low = lax.dot_general(ht[...], dt[...], TT, preferred_element_type=F32)
@@ -210,6 +209,15 @@
 
     wo_copy = remote(wo.at[1 - core], wo_in, wo_send, wo_recv, partner)
     wo_copy.start()
+
+    for copy in pool:
+        copy.wait()
+
+    def turn_keys(b, c):
+        kbuf[b] = jnp.transpose(kbuf[b].reshape(toks // 2, 2 * width))
+        return c
+
+    lax.fori_loop(0, blocks, turn_keys, 0, unroll=4)
 
     def a2_copy(t, s):
         return remote(sum_a.at[t], end_a.at[s], a2_send.at[t], a2_recv.at[s], (row, 2 * (x * SIDE + t) + core))
@@ -282,17 +290,13 @@
         q_copy(chip_by(i, 1), chip).start()
     q_relay(chip, core).start()
 
-    def regroup(b, c):
-        kbuf[b] = jnp.transpose(kbuf[b].reshape(toks // 2, 2 * width))
+    def turn_values(b, c):
         both = vbuf[b].reshape(toks // 2, 2 * width)
         vbuf[b, :toks // 2] = both[:, :width]
         vbuf[b, toks // 2:] = both[:, width:]
         return c
 
-    share = blocks // chips
-    for copy in pool:
-        copy.wait()
-    lax.fori_loop(0, share, regroup, 0, unroll=4)
+    lax.fori_loop(0, blocks, turn_values, 0, unroll=4)
 
     def pair_sent(d, c):
         pair_copy(d).wait_send()
@@ -308,12 +312,10 @@
     for copy in tables:
         copy.wait()
 
-    for i in far[::-1]:
+    for i in far:
         s = chip_by(i, -1)
         q_copy(s, s).wait_recv()
         q_relay(s, core).start()
-        at = (1 + far.index(i)) * share
-        lax.fori_loop(at, at + share, regroup, 0, unroll=4)
 
     def q_landed(d, c):
         q_relay(d, 1 - core).wait_recv()

time: 74.5 us -> 70.4 us (0.945)
  Pallas kernels: 72.3 us -> 68.3 us
    pallas_call x1, Pallas kernels: 72.3 us -> 68.3 us  [run(): pl.pallas_call(kernel, out_shape=jax.ShapeDtypeStruct((rows // planes, co...]
where the time goes in v5:
time: 70.4 us; the launch traced here: 70.2 us
  Pallas kernels  68.3 us (97%)
  local copies, waits for them, and re-layouts  1.38 us (2%)
    pallas_call x1, Pallas kernels, run(): pl.pallas_call(kernel, out_shape=jax.ShapeDtypeStruct((rows // planes, co...  68.3 us

profile of v5, /device:TPU:1, one launch (start us, length us, event | category | flops | bytes accessed | tf_op | source)
XLA Modules:
  0.0 70.2 jit_solution(1642247534963738872)
XLA Ops:
  0.0 0.6 maximum_bitcast_fusion.freq_h
  0.6 68.3 %decode.1 = bf16[64,160]{1,0:T(8,128)(2,1)} custom-call(bf16[160,256]{1,0:T(8,128)(2,1)} %bitcast.16, bf16[160,2048]{1,0:T(8,128)(2,1)} %w_h.1, bf16[512,160]{1,0:T(8,128)(2,1)} %bitcast.15, f32[32,16,2048]{2,1,0:T(8,128)} %up_h.1, f32[1,128]{1,0:T(1,128)} %bitcast.18, f32[1,128]{1,0:T(1,128)} %maximum_bitcast_fusion.freq_h, s32[8,32]{1,0:T(8,128)} %holder_h.1, ...), custom_call_target="tpu_custom_call" | custom-call | tf_op jit(solution)/shard_map/decode/pallas_call | solution.py:525
  68.9 1.4 %copy.15 = bf16[64,160]{1,0:T(8,128)(2,1)} copy(bf16[64,160]{1,0:T(8,128)(2,1)} %decode.1) | data formatting | bytes 40960
  (1 shorter events, 0.0 us)

commit v6 on v5

--- a/solution.py
+++ b/solution.py
@@ -3,6 +3,7 @@
 
 import jax
 import jax.numpy as jnp
+import numpy as np
 from jax import lax
 from jax.experimental import pallas as pl
 from jax.experimental.pallas import tpu as pltpu
@@ -94,7 +95,7 @@
 
 def kernel(ht_h, w_h, dt_h, up_h, gain_h, freq_h, holder_h, index_h, used_h, tenant_h, held_h, k_h, v_h, wo_h,
            out_ref,
-           ht, w, dt, up, gain, freq, holder, index, used, tenant, held, tenant_s, held_s, kbuf, vbuf, wo, wo_in,
+           ht, w, dt, up, gain, freq, holder, index, used, tenant, held, tenant_s, held_s, kbuf, vbuf, wo, wo_in, wo_t,
            part, pair, mine_a, mine_b, land_a, land_b, sum_a, sum_b, end_a, end_b, total, low_t, turned,
            ent_send, ent, tab_v, slot_v, tab, slot_s, q, o_st, e_st,
            partial, tops, partial_in, tops_in, merged, tops_out, parts, tops_all, flat, attended, terms, summed,
@@ -238,19 +239,6 @@
     for o in (2, 1, 3):
         b2_copy((x + o) % SIDE, x).start()
 
-    def ent_wait(i, c):
-        t = (me + peers - i) % peers
-        ent_copy(t, t).wait_recv()
-        return c
-
-    lax.fori_loop(1, peers, ent_wait, 0)
-    table, by_slot = order_entries(ent[...], blocks, rows, tab.shape[1], 2 * cap)
-    tab_v[...] = table
-    slot_v[...] = by_slot
-    tables = (pltpu.make_async_copy(tab_v, tab, tab_sem.at[0]), pltpu.make_async_copy(slot_v, slot_s, tab_sem.at[1]))
-    for copy in tables:
-        copy.start()
-
     for o in steps:
         a2_copy((y + SIDE - o) % SIDE, (y + SIDE - o) % SIDE).wait_recv()
     total[:, :wide_a] = sum_a[y] + end_a[(y + 1) % SIDE] + end_a[(y + 2) % SIDE] + end_a[(y + 3) % SIDE]
@@ -298,6 +286,19 @@
 
     lax.fori_loop(0, blocks, turn_values, 0, unroll=4)
 
+    def ent_wait(i, c):
+        t = (me + peers - i) % peers
+        ent_copy(t, t).wait_recv()
+        return c
+
+    lax.fori_loop(1, peers, ent_wait, 0)
+    table, by_slot = order_entries(ent[...], blocks, rows, tab.shape[1], 2 * cap)
+    tab_v[...] = table
+    slot_v[...] = by_slot
+    tables = (pltpu.make_async_copy(tab_v, tab, tab_sem.at[0]), pltpu.make_async_copy(slot_v, slot_s, tab_sem.at[1]))
+    for copy in tables:
+        copy.start()
+
     def pair_sent(d, c):
         pair_copy(d).wait_send()
         return c
@@ -309,8 +310,6 @@
             b_copy((y + o) % SIDE, i, y).wait_send()
         a2_copy((y + o) % SIDE, y).wait_send()
         b2_copy((x + o) % SIDE, x).wait_send()
-    for copy in tables:
-        copy.wait()
 
     for i in far:
         s = chip_by(i, -1)
@@ -322,6 +321,8 @@
         return c
 
     lax.fori_loop(0, chips, q_landed, 0)
+    for copy in tables:
+        copy.wait()
 
     coef = math.log2(math.e) / math.sqrt(width)
     half = heads // 2
@@ -448,6 +449,8 @@
     for copy in x_copies:
         copy.wait_send()
     wo_copy.wait()
+    wo_t[0] = jnp.transpose(wo[core])
+    wo_t[1] = jnp.transpose(wo_in[...])
 
     for i in far[::-1]:
         s = chip_by(i, -1)
@@ -471,26 +474,34 @@
         at = pl.ds(s * pair_rows, pair_rows)
         return remote(attended.at[at], attended.at[at], ag2_send.at[d], ag2_recv.at[s], (row, 2 * d + core))
 
-    for i in far:
+    by_row = [SIDE * ox + oy for ox in hops for oy in hops]
+    for i in by_row[:-1]:
         at_copy(chip_by(i, 1), chip).start()
     for k, i in enumerate(far):
         t_copy(k, chip_by(i, 1), chip).wait_send()
         p_copy(k, chip_by(i, 1), chip).wait_send()
-    for i in far[::-1]:
-        s = chip_by(i, -1)
-        at_copy(s, s).wait_recv()
     out_rows = out_ref.shape[0]
 
     def z_copy(c, z, s):
         return remote(terms.at[c, pl.ds(z * out_rows, out_rows)], summed.at[c, s], z_send.at[c, z], z_recv.at[c, s],
                       (z, partner[1] if c else me))
 
-    terms[1] = lax.dot_general(attended[...], wo_in[...], NT, preferred_element_type=F32).astype(BF16)
-    for i in (2, 1, 3, 0):
-        z_copy(1, (row + i) % planes, row).start()
-    terms[0] = lax.dot_general(attended[...], wo[core], NT, preferred_element_type=F32).astype(BF16)
-    for i in (2, 1, 3):
-        z_copy(0, (row + i) % planes, row).start()
+    for ox in hops:
+        for oy in hops:
+            if ox or oy:
+                s = chip_by(SIDE * ox + oy, -1)
+                at_copy(s, s).wait_recv()
+        z = (x + SIDE - ox) % SIDE
+        at = pl.ds(z * out_rows, out_rows)
+        some = attended[at, :]
+        terms[1, at, :] = jnp.dot(some, wo_t[1], preferred_element_type=F32).astype(BF16)
+        z_copy(1, z, row).start()
+        terms[0, at, :] = jnp.dot(some, wo_t[0], preferred_element_type=F32).astype(BF16)
+
+        @pl.when(z != row)
+        def _():
+            z_copy(0, z, row).start()
+
     for i in far:
         at_copy(chip_by(i, 1), chip).wait_send()
 
@@ -500,7 +511,7 @@
             z = (row + i) % planes
             z_copy(c, z, z).wait_recv()
             result += summed[c, z].astype(F32)
-    out_ref[...] = result.astype(BF16)
+    out_ref[...] = result
     for c in (1, 0):
         for i in range(c ^ 1, planes):
             z_copy(c, (row + i) % planes, row).wait_send()
@@ -524,12 +535,12 @@
     args = (ht, w, dt, up, gain, freq, holder, index, used, tenant, held, k, v, wo)
     return pl.pallas_call(
         kernel,
-        out_shape=jax.ShapeDtypeStruct((rows // planes, cols), BF16),
+        out_shape=jax.ShapeDtypeStruct((rows // planes, cols), F32),
         in_specs=[pl.BlockSpec(memory_space=pltpu.HBM)] * len(args),
         out_specs=pl.BlockSpec(memory_space=pltpu.VMEM),
         scratch_shapes=[vm(a.shape, a.dtype) for a in args[:11]] + [
             pltpu.SMEM(tenant.shape, I32), pltpu.SMEM(held.shape, I32),
-            vm(k.shape, BF16), vm(v.shape, BF16), vm((2, cols, wide // 2), BF16), vm((cols, wide // 2), BF16),
+            vm(k.shape, BF16), vm(v.shape, BF16), vm((2, cols, wide // 2), BF16), vm((cols, wide // 2), BF16), vm((2, wide // 2, cols), BF16),
             vm((rows, wide + 128), F32), vm((chips, own, wide + 128), F32),
             vm((SIDE, SIDE, own, wide_a), F32), vm((SIDE, SIDE, own, wide_b), F32),
             vm((SIDE, SIDE, own, wide_a), F32), vm((SIDE, SIDE, own, wide_b), F32),
@@ -565,13 +576,13 @@
     width = query_norm_gain.shape[0]
     blocks, toks, kv_heads, _ = paged_key_cache.shape
     half = width // 2
-    freq = ROPE_BASE ** (-(jnp.arange(half, dtype=jnp.float32) * 2.0) / width)
-    freq = jnp.concatenate([freq, freq])[None, :]
+    freq = (ROPE_BASE ** (-(np.arange(half) * 2.0) / width)).astype(np.float32)
+    freq = jnp.asarray(np.concatenate([freq, freq])[None, :])
     down = jnp.transpose(adapter_down_weight, (0, 2, 1)).reshape(count * rank, -1)
     pool = (blocks, toks * kv_heads, width)
     return run(hidden.T, query_weight, down, adapter_up_weight, query_norm_gain[None, :], freq, holder,
                holder_block_index, block_used_length, tenant[None, :], tenant_adapter[None, :],
-               paged_key_cache.reshape(pool), paged_value_cache.reshape(pool), output_weight.T, peers, planes)
+               paged_key_cache.reshape(pool), paged_value_cache.reshape(pool), output_weight.T, peers, planes).astype(BF16)
 
 
 def solution(mesh):

time: 70.4 us -> 71.5 us (1.016)
  Pallas kernels: 68.3 us -> 69.9 us
  local copies, waits for them, and re-layouts: 1.38 us -> 0 us
  other arithmetic: 0.6 us -> 1.46 us
    pallas_call x1, Pallas kernels: 68.3 us -> 69.9 us  [run(): pl.pallas_call(kernel, out_shape=jax.ShapeDtypeStruct((rows // planes, co...]
    convert_element_type x0 -> x1, other arithmetic: none -> 1.46 us  [local(): return run(hidden.T, query_weight, down, adapter_up_weight, query_norm_ga...]
    unnamed x1 -> x0, local copies, waits for them, and re-layouts: 1.38 us -> none
where the time goes in v6:
time: 71.5 us; the launch traced here: 71.3 us
  Pallas kernels  69.9 us (98%)
  other arithmetic  1.46 us (2%)
    pallas_call x1, Pallas kernels, run(): pl.pallas_call(kernel, out_shape=jax.ShapeDtypeStruct((rows // planes, co...  69.9 us
    convert_element_type x1, other arithmetic, local(): return run(hidden.T, query_weight, down, adapter_up_weight, query_norm_ga...  1.46 us

profile of v6, /device:TPU:1, one launch (start us, length us, event | category | flops | bytes accessed | tf_op | source)
XLA Modules:
  0.0 71.3 jit_solution(9913632013764104852)
XLA Ops:
  0.0 69.9 %decode.1 = f32[64,160]{1,0:T(8,128)} custom-call(bf16[160,256]{1,0:T(8,128)(2,1)} %bitcast.14, bf16[160,2048]{1,0:T(8,128)(2,1)} %w_h.1, bf16[512,160]{1,0:T(8,128)(2,1)} %bitcast.13, f32[32,16,2048]{2,1,0:T(8,128)} %up_h.1, f32[1,128]{1,0:T(1,128)} %bitcast.16, f32[1,128]{1,0:T(1,128)} %constant.2.clone.freq_h, s32[8,32]{1,0:T(8,128)} %holder_h.1, ...), custom_call_target="tpu_custom_call" | custom-call | tf_op jit(solution)/shard_map/decode/pallas_call | solution.py:536
  69.9 1.5 %convert_element_type.3 = bf16[64,160]{1,0:T(8,128)(2,1)} convert(f32[64,160]{1,0:T(8,128)} %decode.1) | non-fusion elementwise | flops 10240 | bytes 61440 | tf_op jit(solution)/shard_map/convert_element_type | solution.py:585

commit v7 on v6

--- a/solution.py
+++ b/solution.py
@@ -98,7 +98,7 @@
            ht, w, dt, up, gain, freq, holder, index, used, tenant, held, tenant_s, held_s, kbuf, vbuf, wo, wo_in, wo_t,
            part, pair, mine_a, mine_b, land_a, land_b, sum_a, sum_b, end_a, end_b, total, low_t, turned,
            ent_send, ent, tab_v, slot_v, tab, slot_s, q, o_st, e_st,
-           partial, tops, partial_in, tops_in, merged, tops_out, parts, tops_all, flat, attended, terms, summed,
+           partial, tops, partial_in, tops_in, merged, tops_out, parts, tops_all, attended, terms, summed,
            in_sem, kv_sem, tab_sem, pair_send, pair_recv, a_send, a_recv, b_send, b_recv, a2_send, a2_recv,
            b2_send, b2_recv, en_send, en_recv, ag_send, ag_recv, fw_send, fw_recv,
            wo_send, wo_recv, x_send, x_recv, p_send, p_recv, t_send, t_recv, ag2_send, ag2_recv, z_send, z_recv):
@@ -261,10 +261,16 @@
     q[pl.ds(me * own, own)] = turned[...].astype(BF16)
 
     def chip_by(i, sign):
-        dx, dy = i // SIDE, i % SIDE
-        return ((x + sign * dx + SIDE) % SIDE) * SIDE + (y + sign * dy + SIDE) % SIDE
-
-    far = sorted(range(1, chips), key=lambda i: -(min(i // SIDE, SIDE - i // SIDE) + min(i % SIDE, SIDE - i % SIDE)))
+        i = lax.rem(5 * i, chips)
+        dx, dy = lax.div(i, SIDE), lax.rem(i, SIDE)
+        return (lax.rem(x + sign * dx + SIDE, SIDE)) * SIDE + lax.rem(y + sign * dy + SIDE, SIDE)
+
+    def each(first, last, do):
+        def step(i, c):
+            do(i)
+            return c
+
+        lax.fori_loop(first, last, step, 0)
 
     def q_copy(d, s):
         at = pl.ds((2 * s + core) * own, own)
@@ -274,8 +280,7 @@
         at = pl.ds((2 * s + c) * own, own)
         return remote(q.at[at], q.at[at], fw_send.at[s], fw_recv.at[s], partner)
 
-    for i in far:
-        q_copy(chip_by(i, 1), chip).start()
+    each(1, chips, lambda i: q_copy(chip_by(i, 1), chip).start())
     q_relay(chip, core).start()
 
     def turn_values(b, c):
@@ -311,10 +316,12 @@
         a2_copy((y + o) % SIDE, y).wait_send()
         b2_copy((x + o) % SIDE, x).wait_send()
 
-    for i in far:
+    def relay(i):
         s = chip_by(i, -1)
         q_copy(s, s).wait_recv()
         q_relay(s, core).start()
+
+    each(1, chips, relay)
 
     def q_landed(d, c):
         q_relay(d, 1 - core).wait_recv()
@@ -360,8 +367,8 @@
     lax.fori_loop(0, tab.shape[1] // (GROUP * UNROLL), chunks, 0)
 
     lane = iota((half, 128), 1)
-    same_head = (lane & (half - 1)) == iota((half, 128), 0)
-    lane_row = jnp.where(same_head, lax.div(lane, half), -2)
+    same_head = lax.div(lane, 128 // half) == iota((half, 128), 0)
+    lane_row = jnp.where(same_head, lane & (128 // half - 1), -2)
     slots = 2 * cap
 
     def merge(d, hv):
@@ -396,7 +403,7 @@
         n = fs.shape[0]
         return jnp.transpose(jnp.concatenate([fs, jnp.zeros((128 - n, 128), F32)], axis=0))
 
-    order = far + [0]
+    order = [*range(1, chips), 0]
     x_copies[0].wait_recv()
     t0 = jnp.concatenate([tops[core, pl.ds(chip_by(i, 1), 1), :] for i in order], axis=0)
     t1 = jnp.concatenate([tops_in[pl.ds(chip_by(i, 1), 1), :] for i in order], axis=0)
@@ -411,23 +418,26 @@
     def t_copy(k, d, s):
         return remote(tops_out.at[k], tops_all.at[s], t_send.at[k], t_recv.at[s], (row, 2 * d + core))
 
-    def p_copy(k, d, s):
-        return remote(merged.at[k], parts.at[s], p_send.at[k], p_recv.at[s], (row, 2 * d + core))
-
-    for k, i in enumerate(order):
-        if i:
-            t_copy(k, chip_by(i, 1), chip).start()
+    part_rows = 128 // 2
+
+    def p_copy(n, k, d, s):
+        at = pl.ds(n * part_rows, part_rows)
+        return remote(merged.at[k, at], parts.at[s, at], p_send.at[n, k], p_recv.at[n, s], (row, 2 * d + core))
+
+    each(1, chips, lambda i: t_copy(i - 1, chip_by(i, 1), chip).start())
     x_copies[1].wait_recv()
-    for k, i in enumerate(order):
-        d = chip_by(i, 1)
-        both = (f[:, k:k + 1] * partial[core, d].astype(F32)
-                + f[:, chips + k:chips + k + 1] * partial_in[d].astype(F32)).astype(BF16)
-        if i:
-            merged[k] = both
-            p_copy(k, d, chip).start()
-        else:
-            parts[chip] = both
-            tops_all[chip] = tops_out[k]
+    for n in range(2):
+        at = slice(n * part_rows, (n + 1) * part_rows)
+        for k, i in enumerate(order):
+            d = chip_by(i, 1)
+            both = (f[at, k:k + 1] * partial[core, d, at].astype(F32)
+                    + f[at, chips + k:chips + k + 1] * partial_in[d, at].astype(F32)).astype(BF16)
+            if i:
+                merged[k, at] = both
+                p_copy(n, k, d, chip).start()
+            else:
+                parts[chip, at] = both
+    tops_all[chip] = tops_out[chips - 1]
 
     def ent_sent(i, c):
         ent_copy((me + i) % peers, me).wait_send()
@@ -452,58 +462,50 @@
     wo_t[0] = jnp.transpose(wo[core])
     wo_t[1] = jnp.transpose(wo_in[...])
 
-    for i in far[::-1]:
-        s = chip_by(i, -1)
-        t_copy(0, s, s).wait_recv()
+    each(0, chips - 1, lambda i: t_copy(0, chip_by(i + 1, -1), chip_by(i + 1, -1)).wait_recv())
     top = tops_all[:, 0, :]
     f = jnp.exp2(top - jnp.max(top, axis=0, keepdims=True))
     f = columns(f / jnp.sum(f, axis=0, keepdims=True))
-    for i in far[::-1]:
-        s = chip_by(i, -1)
-        p_copy(0, s, s).wait_recv()
-    acc = jnp.zeros((128, width), F32)
-    for s in range(chips):
-        acc += f[:, s:s + 1] * parts[s].astype(F32)
-    flat[...] = acc
     pair_rows = 2 * own
-    here = pl.ds(chip * pair_rows, pair_rows)
-    for h in range(half):
-        attended[here, h * width:(h + 1) * width] = flat[pl.ds(h, pair_rows, stride=half), :].astype(BF16)
-
-    def at_copy(d, s):
-        at = pl.ds(s * pair_rows, pair_rows)
-        return remote(attended.at[at], attended.at[at], ag2_send.at[d], ag2_recv.at[s], (row, 2 * d + core))
-
-    by_row = [SIDE * ox + oy for ox in hops for oy in hops]
-    for i in by_row[:-1]:
-        at_copy(chip_by(i, 1), chip).start()
-    for k, i in enumerate(far):
-        t_copy(k, chip_by(i, 1), chip).wait_send()
-        p_copy(k, chip_by(i, 1), chip).wait_send()
+    cols = half * width // 2
+
+    def at_copy(n, d, s):
+        at = attended.at[pl.ds(s * pair_rows, pair_rows), pl.ds(n * cols, cols)]
+        return remote(at, at, ag2_send.at[n, d], ag2_recv.at[n, s], (row, 2 * d + core))
+
+    for n in range(2):
+        each(1, chips, lambda i: p_copy(n, 0, chip_by(i, -1), chip_by(i, -1)).wait_recv())
+        at = slice(n * part_rows, (n + 1) * part_rows)
+        acc = jnp.zeros((part_rows, width), F32)
+        for s in range(chips):
+            acc += f[at, s:s + 1] * parts[s, at].astype(F32)
+        acc = acc.astype(BF16)
+        for h in range(half // 2):
+            attended[pl.ds(chip * pair_rows, pair_rows), n * cols + h * width:n * cols + (h + 1) * width] = (
+                acc[h * pair_rows:(h + 1) * pair_rows])
+        each(1, chips, lambda i: at_copy(n, chip_by(i, 1), chip).start())
+
+    def merged_sent(i):
+        t_copy(i - 1, chip_by(i, 1), chip).wait_send()
+        for n in range(2):
+            p_copy(n, i - 1, chip_by(i, 1), chip).wait_send()
+
+    each(1, chips, merged_sent)
+
     out_rows = out_ref.shape[0]
 
     def z_copy(c, z, s):
         return remote(terms.at[c, pl.ds(z * out_rows, out_rows)], summed.at[c, s], z_send.at[c, z], z_recv.at[c, s],
                       (z, partner[1] if c else me))
 
-    for ox in hops:
-        for oy in hops:
-            if ox or oy:
-                s = chip_by(SIDE * ox + oy, -1)
-                at_copy(s, s).wait_recv()
-        z = (x + SIDE - ox) % SIDE
-        at = pl.ds(z * out_rows, out_rows)
-        some = attended[at, :]
-        terms[1, at, :] = jnp.dot(some, wo_t[1], preferred_element_type=F32).astype(BF16)
-        z_copy(1, z, row).start()
-        terms[0, at, :] = jnp.dot(some, wo_t[0], preferred_element_type=F32).astype(BF16)
-
-        @pl.when(z != row)
-        def _():
-            z_copy(0, z, row).start()
-
-    for i in far:
-        at_copy(chip_by(i, 1), chip).wait_send()
+    for n in range(2):
+        each(1, chips, lambda i: at_copy(n, chip_by(i, -1), chip_by(i, -1)).wait_recv())
+    for c in (1, 0):
+        terms[c] = jnp.dot(attended[...], wo_t[c], preferred_element_type=F32).astype(BF16)
+        for i in (2, 1, 3, 0)[:3 + c]:
+            z_copy(c, (row + i) % planes, row).start()
+    for n in range(2):
+        each(1, chips, lambda i: at_copy(n, chip_by(i, 1), chip).wait_send())
 
     result = terms[0, pl.ds(row * out_rows, out_rows), :].astype(F32)
     for c in (1, 0):
@@ -511,7 +513,7 @@
             z = (row + i) % planes
             z_copy(c, z, z).wait_recv()
             result += summed[c, z].astype(F32)
-    out_ref[...] = result
+    out_ref[...] = result.astype(BF16)
     for c in (1, 0):
         for i in range(c ^ 1, planes):
             z_copy(c, (row + i) % planes, row).wait_send()
@@ -535,7 +537,7 @@
     args = (ht, w, dt, up, gain, freq, holder, index, used, tenant, held, k, v, wo)
     return pl.pallas_call(
         kernel,
-        out_shape=jax.ShapeDtypeStruct((rows // planes, cols), F32),
+        out_shape=jax.ShapeDtypeStruct((rows // planes, cols), BF16),
         in_specs=[pl.BlockSpec(memory_space=pltpu.HBM)] * len(args),
         out_specs=pl.BlockSpec(memory_space=pltpu.VMEM),
         scratch_shapes=[vm(a.shape, a.dtype) for a in args[:11]] + [
@@ -554,14 +556,15 @@
             vm((2, chips, 128, width), BF16), vm((2, chips, 128), F32),
             vm((chips, 128, width), BF16), vm((chips, 128), F32),
             vm((chips, 128, width), BF16), vm((chips, 8, 128), F32),
-            vm((chips, 128, width), BF16), vm((chips, 8, 128), F32), vm((128, width), F32),
-            vm((rows, wide // 2), BF16), vm((2, rows, cols), BF16), vm((2, planes, rows // planes, cols), BF16),
+            vm((chips, 128, width), BF16), vm((chips, 8, 128), F32), vm((rows, wide // 2), BF16),
+            vm((2, rows, cols), BF16), vm((2, planes, rows // planes, cols), BF16),
             dma((15,)), dma((2 * PIECES,)), dma((2,)), dma((chips,)), dma((chips,)),
             dma((SIDE,)), dma((SIDE,)), dma((SIDE, SIDE)), dma((SIDE, SIDE)),
             dma((SIDE,)), dma((SIDE,)), dma((SIDE,)), dma((SIDE,)),
             dma((peers,)), dma((peers,)), dma((chips,)), dma((chips,)), dma((chips,)), dma((chips,)),
-            dma, dma, dma((2,)), dma((2,)), dma((chips,)), dma((chips,)), dma((chips,)), dma((chips,)),
-            dma((chips,)), dma((chips,)), dma((2, planes)), dma((2, planes)),
+            dma, dma, dma((2,)), dma((2,)),
+            dma((2, chips)), dma((2, chips)), dma((chips,)), dma((chips,)),
+            dma((2, chips)), dma((2, chips)), dma((2, planes)), dma((2, planes)),
         ],
         compiler_params=pltpu.CompilerParams(
             vmem_limit_bytes=62 * 2**20, collective_id=0, has_side_effects=True),
@@ -582,7 +585,7 @@
     pool = (blocks, toks * kv_heads, width)
     return run(hidden.T, query_weight, down, adapter_up_weight, query_norm_gain[None, :], freq, holder,
                holder_block_index, block_used_length, tenant[None, :], tenant_adapter[None, :],
-               paged_key_cache.reshape(pool), paged_value_cache.reshape(pool), output_weight.T, peers, planes).astype(BF16)
+               paged_key_cache.reshape(pool), paged_value_cache.reshape(pool), output_weight.T, peers, planes)
 
 
 def solution(mesh):

time: 71.5 us -> 70 us (0.979)
  Pallas kernels: 69.9 us -> 68.4 us
  other arithmetic: 1.46 us -> 0 us
  local copies, waits for them, and re-layouts: 0 us -> 1.38 us
    pallas_call x1, Pallas kernels: 69.9 us -> 68.4 us  [run(): pl.pallas_call(kernel, out_shape=jax.ShapeDtypeStruct((rows // planes, co...]
    convert_element_type x1 -> x0, other arithmetic: 1.46 us -> none  [local(): return run(hidden.T, query_weight, down, adapter_up_weight, query_norm_ga...]
    unnamed x0 -> x1, local copies, waits for them, and re-layouts: none -> 1.38 us
where the time goes in v7:
time: 70 us; the launch traced here: 69.8 us
  Pallas kernels  68.4 us (98%)
  local copies, waits for them, and re-layouts  1.38 us (2%)
    pallas_call x1, Pallas kernels, run(): pl.pallas_call(kernel, out_shape=jax.ShapeDtypeStruct((rows // planes, co...  68.4 us

profile of v7, /device:TPU:1, one launch (start us, length us, event | category | flops | bytes accessed | tf_op | source)
XLA Modules:
  0.0 69.8 jit_solution(15934807889482724066)
XLA Ops:
  0.0 68.4 %decode.1 = bf16[64,160]{1,0:T(8,128)(2,1)} custom-call(bf16[160,256]{1,0:T(8,128)(2,1)} %bitcast.14, bf16[160,2048]{1,0:T(8,128)(2,1)} %w_h.1, bf16[512,160]{1,0:T(8,128)(2,1)} %bitcast.13, f32[32,16,2048]{2,1,0:T(8,128)} %up_h.1, f32[1,128]{1,0:T(1,128)} %bitcast.16, f32[1,128]{1,0:T(1,128)} %constant.2.clone.freq_h, s32[8,32]{1,0:T(8,128)} %holder_h.1, ...), custom_call_target="tpu_custom_call" | custom-call | tf_op jit(solution)/shard_map/decode/pallas_call | solution.py:538
  68.4 1.4 %copy.16 = bf16[64,160]{1,0:T(8,128)(2,1)} copy(bf16[64,160]{1,0:T(8,128)(2,1)} %decode.1) | data formatting | bytes 40960

commit v8 on v7

--- a/solution.py
+++ b/solution.py
@@ -261,9 +261,13 @@
     q[pl.ds(me * own, own)] = turned[...].astype(BF16)
 
     def chip_by(i, sign):
-        i = lax.rem(5 * i, chips)
-        dx, dy = lax.div(i, SIDE), lax.rem(i, SIDE)
-        return (lax.rem(x + sign * dx + SIDE, SIDE)) * SIDE + lax.rem(y + sign * dy + SIDE, SIDE)
+        dx, dy = i // SIDE, i % SIDE
+        return ((x + sign * dx + SIDE) % SIDE) * SIDE + (y + sign * dy + SIDE) % SIDE
+
+    far = sorted(range(1, chips), key=lambda i: -(min(i // SIDE, SIDE - i // SIDE) + min(i % SIDE, SIDE - i % SIDE)))
+
+    def turn(i):
+        return lax.rem(chip + i, chips)
 
     def each(first, last, do):
         def step(i, c):
@@ -280,7 +284,8 @@
         at = pl.ds((2 * s + c) * own, own)
         return remote(q.at[at], q.at[at], fw_send.at[s], fw_recv.at[s], partner)
 
-    each(1, chips, lambda i: q_copy(chip_by(i, 1), chip).start())
+    for i in far:
+        q_copy(chip_by(i, 1), chip).start()
     q_relay(chip, core).start()
 
     def turn_values(b, c):
@@ -316,12 +321,11 @@
         a2_copy((y + o) % SIDE, y).wait_send()
         b2_copy((x + o) % SIDE, x).wait_send()
 
-    def relay(i):
+    for i in far:
         s = chip_by(i, -1)
         q_copy(s, s).wait_recv()
         q_relay(s, core).start()
 
-    each(1, chips, relay)
 
     def q_landed(d, c):
         q_relay(d, 1 - core).wait_recv()
@@ -403,7 +407,7 @@
         n = fs.shape[0]
         return jnp.transpose(jnp.concatenate([fs, jnp.zeros((128 - n, 128), F32)], axis=0))
 
-    order = [*range(1, chips), 0]
+    order = far + [0]
     x_copies[0].wait_recv()
     t0 = jnp.concatenate([tops[core, pl.ds(chip_by(i, 1), 1), :] for i in order], axis=0)
     t1 = jnp.concatenate([tops_in[pl.ds(chip_by(i, 1), 1), :] for i in order], axis=0)
@@ -424,7 +428,8 @@
         at = pl.ds(n * part_rows, part_rows)
         return remote(merged.at[k, at], parts.at[s, at], p_send.at[n, k], p_recv.at[n, s], (row, 2 * d + core))
 
-    each(1, chips, lambda i: t_copy(i - 1, chip_by(i, 1), chip).start())
+    for k, i in enumerate(far):
+        t_copy(k, chip_by(i, 1), chip).start()
     x_copies[1].wait_recv()
     for n in range(2):
         at = slice(n * part_rows, (n + 1) * part_rows)
@@ -462,7 +467,7 @@
     wo_t[0] = jnp.transpose(wo[core])
     wo_t[1] = jnp.transpose(wo_in[...])
 
-    each(0, chips - 1, lambda i: t_copy(0, chip_by(i + 1, -1), chip_by(i + 1, -1)).wait_recv())
+    each(1, chips, lambda i: t_copy(0, turn(i), turn(i)).wait_recv())
     top = tops_all[:, 0, :]
     f = jnp.exp2(top - jnp.max(top, axis=0, keepdims=True))
     f = columns(f / jnp.sum(f, axis=0, keepdims=True))
@@ -474,7 +479,7 @@
         return remote(at, at, ag2_send.at[n, d], ag2_recv.at[n, s], (row, 2 * d + core))
 
     for n in range(2):
-        each(1, chips, lambda i: p_copy(n, 0, chip_by(i, -1), chip_by(i, -1)).wait_recv())
+        each(1, chips, lambda i: p_copy(n, 0, turn(i), turn(i)).wait_recv())
         at = slice(n * part_rows, (n + 1) * part_rows)
         acc = jnp.zeros((part_rows, width), F32)
         for s in range(chips):
@@ -483,12 +488,13 @@
         for h in range(half // 2):
             attended[pl.ds(chip * pair_rows, pair_rows), n * cols + h * width:n * cols + (h + 1) * width] = (
                 acc[h * pair_rows:(h + 1) * pair_rows])
-        each(1, chips, lambda i: at_copy(n, chip_by(i, 1), chip).start())
+        for i in far:
+            at_copy(n, chip_by(i, 1), chip).start()
 
     def merged_sent(i):
-        t_copy(i - 1, chip_by(i, 1), chip).wait_send()
+        t_copy(i - 1, turn(i), chip).wait_send()
         for n in range(2):
-            p_copy(n, i - 1, chip_by(i, 1), chip).wait_send()
+            p_copy(n, i - 1, turn(i), chip).wait_send()
 
     each(1, chips, merged_sent)
 
@@ -499,13 +505,13 @@
                       (z, partner[1] if c else me))
 
     for n in range(2):
-        each(1, chips, lambda i: at_copy(n, chip_by(i, -1), chip_by(i, -1)).wait_recv())
+        each(1, chips, lambda i: at_copy(n, turn(i), turn(i)).wait_recv())
     for c in (1, 0):
         terms[c] = jnp.dot(attended[...], wo_t[c], preferred_element_type=F32).astype(BF16)
         for i in (2, 1, 3, 0)[:3 + c]:
             z_copy(c, (row + i) % planes, row).start()
     for n in range(2):
-        each(1, chips, lambda i: at_copy(n, chip_by(i, 1), chip).wait_send())
+        each(1, chips, lambda i: at_copy(n, turn(i), chip).wait_send())
 
     result = terms[0, pl.ds(row * out_rows, out_rows), :].astype(F32)
     for c in (1, 0):

time: 70 us -> 68.2 us (0.974)
  Pallas kernels: 68.4 us -> 66.6 us
    pallas_call x1, Pallas kernels: 68.4 us -> 66.6 us  [run(): pl.pallas_call(kernel, out_shape=jax.ShapeDtypeStruct((rows // planes, co...]
where the time goes in v8:
time: 68.2 us; the launch traced here: 68 us
  Pallas kernels  66.6 us (98%)
  local copies, waits for them, and re-layouts  1.38 us (2%)
    pallas_call x1, Pallas kernels, run(): pl.pallas_call(kernel, out_shape=jax.ShapeDtypeStruct((rows // planes, co...  66.6 us
    unnamed x1, local copies, waits for them, and re-layouts  1.38 us

profile of v8, /device:TPU:1, one launch (start us, length us, event | category | flops | bytes accessed | tf_op | source)
XLA Modules:
  0.0 68.0 jit_solution(6367945858071462130)
XLA Ops:
  0.0 66.6 %decode.1 = bf16[64,160]{1,0:T(8,128)(2,1)} custom-call(bf16[160,256]{1,0:T(8,128)(2,1)} %bitcast.14, bf16[160,2048]{1,0:T(8,128)(2,1)} %w_h.1, bf16[512,160]{1,0:T(8,128)(2,1)} %bitcast.13, f32[32,16,2048]{2,1,0:T(8,128)} %up_h.1, f32[1,128]{1,0:T(1,128)} %bitcast.16, f32[1,128]{1,0:T(1,128)} %constant.2.clone.freq_h, s32[8,32]{1,0:T(8,128)} %holder_h.1, ...), custom_call_target="tpu_custom_call" | custom-call | tf_op jit(solution)/shard_map/decode/pallas_call | solution.py:544
  66.6 1.4 %copy.16 = bf16[64,160]{1,0:T(8,128)(2,1)} copy(bf16[64,160]{1,0:T(8,128)(2,1)} %decode.1) | data formatting | bytes 40960
